TPU v7x, 32 devices: a whole 2x2x4 slice. The times are simulated.
32 devices in a mesh: groups: 2 (over x), dom: 16 (over z, y, core).
Axes of the slice: x: 2, y: 2, z: 4, core: 2. Of those that a mesh axis runs over, the one named last changes fastest.
Arguments:
- features: bfloat16 [8192, 256], P(('groups', 'dom')), parts along dimension 0, may hold values from -6 to 6
- out_grad: bfloat16 [8192, 256], P(('groups', 'dom')), parts along dimension 0, may hold values from -6 to 6
- send_weight: bfloat16 [256, 256], replicated, may hold values from -0.375 to 0.375
- recv_weight: bfloat16 [256, 256], replicated, may hold values from -0.375 to 0.375
- edge_bias: float32 [256], replicated, may hold values from -1 to 1
- coarse_weight: bfloat16 [256, 256], replicated, may hold values from -0.375 to 0.375
- top_weight: float32 [256, 256], replicated, may hold values from -0.375 to 0.375
- out_weight: bfloat16 [256, 256], replicated, may hold values from -0.375 to 0.375
- edge_sender: int32 [32, 2048], P(('groups', 'dom')), parts along dimension 0, may hold values from 0 to 383
- edge_receiver: int32 [32, 2048], P(('groups', 'dom')), parts along dimension 0, may hold values from 0 to 255
- halo_rows: int32 [32, 4, 32], P(('groups', 'dom')), parts along dimension 0, may hold values from 0 to 255
- owner_slot: int32 [32, 256], P(('groups', 'dom')), parts along dimension 0, may hold values from 0 to 639, as said below
- cluster_index: int32 [32, 256], P(('groups', 'dom')), parts along dimension 0, may hold values from 0 to 15
- slot_coarse: int32 [32, 640], P(('groups', 'dom')), parts along dimension 0, may hold values from 0 to 16, as said below
- coarse_parent: int32 [512], P(('groups', 'dom')), parts along dimension 0, may hold values from 0 to 255
Outputs:
- updated: bfloat16 [8192, 256], P(('groups', 'dom')), parts along dimension 0
- feature_grad: float32 [8192, 256], P(('groups', 'dom')), parts along dimension 0
- send_weight_grad: float32 [512, 256], P('groups'), parts along dimension 0
- recv_weight_grad: float32 [512, 256], P('groups'), parts along dimension 0
- edge_bias_grad: float32 [512], P('groups'), parts along dimension 0
- coarse_weight_grad: float32 [512, 256], P('groups'), parts along dimension 0
- top_weight_grad: float32 [512, 256], P('groups'), parts along dimension 0
- out_weight_grad: float32 [512, 256], P('groups'), parts along dimension 0
There are 2 independent parts, one for each index of `groups`. A program takes and returns all parts, laid end to end along the dimension named above; an argument that names none is the same for every part. Nothing has to cross between parts.
Inputs may be any that keep to these rules, and one draw needn't show every extreme that they name: Within one partition all places differ; the owner of a row is owner_slot // 40; in every draw one owner takes all 40 places of every partition. slot_coarse[o, p * 40 + j] equals cluster_index of the row of partition p whose owner_slot is o * 40 + j, and 16 where no row has that place.
All inputs are finite; a program needn't handle non-finite values.
Results may differ from a plain program's by a relative error of at most 0.0073.
Values may be sent and summed in bfloat16 or wider, within the bound.
A program may use at most 64 MiB of HBM per device.

v0:
```python
import jax
import jax.numpy as jnp
from jax import lax
from jax.sharding import PartitionSpec as P

DEG = 8
PW = 8
NCC = 256


def from_behind(value, axis, by):
    length = lax.axis_size(axis)
    pairs = [(i, i + by) for i in range(length) if 0 <= i + by < length]
    return lax.ppermute(value, axis, pairs)


def silu_grad(values):
    gate = jax.nn.sigmoid(values)
    return gate * (1.0 + values * (1.0 - gate))


def pass_rows(row_values, offset):
    return from_behind(row_values, "dom", offset)


def owner_trade(buffer):
    return lax.all_to_all(buffer, "dom", split_axis=0, concat_axis=0, tiled=True)


def top_total(partial_value):
    return lax.psum(partial_value, "dom")


def contract_first(left, right, precision=None):
    return lax.dot_general(
        left,
        right,
        (((0,), (0,)), ((), ())),
        precision=precision,
        preferred_element_type=jnp.float32,
    )


def contract_last(left, right, precision=None):
    return lax.dot_general(
        left,
        right,
        (((1,), (1,)), ((), ())),
        precision=precision,
        preferred_element_type=jnp.float32,
    )


def shards(
    features,
    out_grad,
    send_weight,
    recv_weight,
    edge_bias,
    coarse_weight,
    top_weight,
    out_weight,
    edge_sender,
    edge_receiver,
    halo_rows,
    owner_slot,
    cluster_index,
    slot_coarse,
    coarse_parent,
):
    highest = lax.Precision.HIGHEST
    domains = lax.axis_size("dom")
    local_rows = features.shape[0]
    feature_width = features.shape[1]
    coarse_rows = coarse_parent.shape[0]
    slot_count = slot_coarse.shape[1]
    offsets = (1, -1, PW, -PW)
    senders = edge_sender[0]
    receivers = edge_receiver[0]
    send_lists = halo_rows[0]
    slot_list = owner_slot[0]
    slots_each = send_lists.shape[1]
    arrivals = []
    for direction, offset in enumerate(offsets):
        arrivals.append(pass_rows(features[send_lists[direction]], offset))
    node_table = jnp.concatenate([features] + arrivals, axis=0)
    table_rows = node_table.shape[0]
    send_proj = jnp.dot(node_table, send_weight, preferred_element_type=jnp.float32)
    recv_proj = jnp.dot(features, recv_weight, preferred_element_type=jnp.float32)
    edge_block = min(senders.shape[0], 2048)
    block_count = senders.shape[0] // edge_block
    sender_blocks = senders.reshape(block_count, edge_block)
    receiver_blocks = receivers.reshape(block_count, edge_block)

    def forward_block(running, block_ids):
        block_senders, block_receivers = block_ids
        pre_act = send_proj[block_senders] + recv_proj[block_receivers] + edge_bias
        return (
            running
            + jax.ops.segment_sum(jax.nn.silu(pre_act), block_receivers, num_segments=local_rows),
            None,
        )

    aggregate, _ = lax.scan(
        forward_block,
        jnp.zeros((local_rows, feature_width), jnp.float32),
        (sender_blocks, receiver_blocks),
    )
    hidden = (features.astype(jnp.float32) + aggregate / DEG).astype(jnp.bfloat16)
    member = (slot_coarse[0][None, :] == jnp.arange(coarse_rows, dtype=jnp.int32)[:, None]).astype(
        jnp.bfloat16
    )

    def gather_up(row_values):
        buffer = jnp.zeros((slot_count, feature_width), jnp.bfloat16).at[slot_list].set(row_values)
        arrived = owner_trade(buffer)
        return jnp.dot(member, arrived, preferred_element_type=jnp.float32)

    def spread_down(coarse_values):
        buffer = contract_first(member, coarse_values).astype(jnp.bfloat16)
        returned = owner_trade(buffer)
        return returned[slot_list]

    coarse = gather_up(hidden) * 0.25
    coarse_low = coarse.astype(jnp.bfloat16)
    coarse_act = jnp.dot(coarse_low, coarse_weight, preferred_element_type=jnp.float32)
    coarse_mid = coarse + jax.nn.silu(coarse_act)
    parent_hot = (coarse_parent[None, :] == jnp.arange(NCC, dtype=jnp.int32)[:, None]).astype(
        jnp.float32
    )
    top_scale = (NCC / (coarse_rows * domains)) ** 0.5
    top_level = top_total(jnp.dot(parent_hot, coarse_mid, precision=highest)) * top_scale
    top_act = jnp.dot(top_level, top_weight, precision=highest)
    coarse_out = (coarse_mid + contract_first(parent_hot, jax.nn.silu(top_act), highest)).astype(
        jnp.bfloat16
    )
    joined = (hidden.astype(jnp.float32) + spread_down(coarse_out).astype(jnp.float32)).astype(
        jnp.bfloat16
    )
    updated = jnp.dot(joined, out_weight, preferred_element_type=jnp.float32).astype(jnp.bfloat16)
    gscale = float(local_rows * domains) ** (-0.5)
    out_term = contract_first(joined, out_grad)
    d_joined = contract_last(out_grad, out_weight).astype(jnp.bfloat16)
    d_coarse_out = gather_up(d_joined)
    d_top_sum = top_total(jnp.dot(parent_hot, d_coarse_out, precision=highest))
    d_top_act = d_top_sum * silu_grad(top_act)
    top_weight_grad = gscale * contract_first(top_level, d_top_act, highest)
    d_top = contract_last(d_top_act, top_weight, highest)
    d_coarse_mid = d_coarse_out + top_scale * contract_first(parent_hot, d_top, highest)
    d_act = (d_coarse_mid * silu_grad(coarse_act)).astype(jnp.bfloat16)
    coarse_term = contract_first(coarse_low, d_act)
    d_coarse = (d_coarse_mid + contract_last(d_act, coarse_weight)).astype(jnp.bfloat16)
    d_hidden = d_joined.astype(jnp.float32) + 0.25 * spread_down(d_coarse).astype(jnp.float32)
    d_aggregate = d_hidden / DEG

    def backward_block(running, block_ids):
        block_senders, block_receivers = block_ids
        bias_sum, send_sum, recv_sum = running
        pre_act = send_proj[block_senders] + recv_proj[block_receivers] + edge_bias
        d_pre = d_aggregate[block_receivers] * silu_grad(pre_act)
        bias_sum = bias_sum + jnp.sum(d_pre, axis=0)
        send_sum = send_sum + jax.ops.segment_sum(d_pre, block_senders, num_segments=table_rows)
        recv_sum = recv_sum + jax.ops.segment_sum(d_pre, block_receivers, num_segments=local_rows)
        return ((bias_sum, send_sum, recv_sum), None)

    initial_sums = (
        jnp.zeros((feature_width,), jnp.float32),
        jnp.zeros((table_rows, feature_width), jnp.float32),
        jnp.zeros((local_rows, feature_width), jnp.float32),
    )
    (bias_sum, send_sum, recv_sum), _ = lax.scan(
        backward_block, initial_sums, (sender_blocks, receiver_blocks)
    )
    d_send_proj = send_sum.astype(jnp.bfloat16)
    d_recv_proj = recv_sum.astype(jnp.bfloat16)
    send_term = contract_first(node_table, d_send_proj)
    recv_term = contract_first(features, d_recv_proj)
    d_table = contract_last(d_send_proj, send_weight)
    d_local = contract_last(d_recv_proj, recv_weight)
    feature_grad = d_hidden + d_table[:local_rows] + d_local
    d_halo = d_table[local_rows:].astype(jnp.bfloat16)
    for direction, offset in enumerate(offsets):
        returned = pass_rows(d_halo[direction * slots_each : (direction + 1) * slots_each], -offset)
        feature_grad = feature_grad.at[send_lists[direction]].add(returned.astype(jnp.float32))
    summed = lax.psum((send_term, recv_term, bias_sum, coarse_term, out_term), "dom")
    return (
        updated,
        feature_grad,
        gscale * summed[0],
        gscale * summed[1],
        gscale * summed[2],
        gscale * summed[3],
        top_weight_grad,
        gscale * summed[4],
    )


def solution(mesh):
    in_specs = (
        P(("groups", "dom"), None),
        P(("groups", "dom"), None),
        P(),
        P(),
        P(),
        P(),
        P(),
        P(),
        P(("groups", "dom"), None),
        P(("groups", "dom"), None),
        P(("groups", "dom"), None, None),
        P(("groups", "dom"), None),
        P(("groups", "dom"), None),
        P(("groups", "dom"), None),
        P(("groups", "dom")),
    )
    out_specs = (
        P(("groups", "dom"), None),
        P(("groups", "dom"), None),
        P("groups", None),
        P("groups", None),
        P("groups"),
        P("groups", None),
        P("groups", None),
        P("groups", None),
    )
    return jax.shard_map(shards, mesh=mesh, in_specs=in_specs, out_specs=out_specs, check_vma=False)
```

profile of v0, /device:TPU:0, one launch (start us, length us, event | category | flops | bytes accessed | tf_op | source)
XLA Modules:
  0.0 358.2 jit_solution(13001273093068734998)
XLA Ops:
  8.1 1.5 gather_fusion.3
  9.6 1.3 collective-permute-start.3
  10.9 1.5 gather_fusion.1
  12.4 1.3 collective-permute-start.1
  13.7 1.5 gather_fusion
  15.3 3.0 collective-permute-start
  18.3 1.5 gather_fusion.2
  19.8 6.3 %collective-permute-start.2 = (bf16[32,256]{1,0:T(8,128)(2,1)S(1)}, bf16[32,256]{1,0:T(8,128)(2,1)S(1)}, u32[]{:S(2)}, u32[]{:S(2)}) collective-permute-start(bf16[32,256]{1,0:T(8,128)(2,1)S(1)} %gather_fusion.2), channel_id=1, source_target_pairs={{0,8},{1,9},{2,10},{3,11},{4,12},{5,13},{6,14},{7,15},{16,24},{17,... | collective-permute-start | bytes 49160 | tf_op jit(solution)/shard_map/ppermute | solution.py:14
  26.8 1.2 convolution_convert_fusion.2
  28.0 2.2 scatter_custom_fusion.2
  30.2 4.6 %all-to-all-start.2 = ((bf16[16,40,256]{2,1,0:T(8,128)(2,1)}), bf16[16,40,256]{2,1,0:T(8,128)(2,1)}, u32[]{:S(2)}, u32[]{:S(2)}) async-start(bf16[16,40,256]{2,1,0:T(8,128)(2,1)} %bitcast.19), calls=%async_computation.2 | async-start | bytes 655360 | tf_op jit(solution)/shard_map/all_to_all | solution.py:27
  36.4 6.6 %gather_fusion.5 = f32[2048,256]{1,0:T(8,128)S(1)} fusion(f32[256,256]{1,0:T(8,128)S(1)} %fusion.57, s32[2048]{0:T(1024)S(1)} %get-tuple-element.77), kind=kCustom, calls=%fused_computation.5 | custom fusion | bytes 4202496 | tf_op jit(solution)/shard_map/while/body/eval_jaxpr/gather | solution.py:97
  43.4 8.6 %gather_fusion.4 = f32[2048,256]{1,0:T(8,128)} fusion(f32[384,256]{1,0:T(8,128)S(1)} %fusion.56, s32[2048]{0:T(1024)S(1)} %get-tuple-element.78), kind=kCustom, calls=%fused_computation.4 | custom fusion | bytes 4202496 | tf_op jit(solution)/shard_map/while/body/eval_jaxpr/gather | solution.py:97
  52.0 12.6 %scatter_custom_fusion = f32[256,256]{1,0:T(8,128)S(1)} fusion(s32[2048]{0:T(1024)} %bitcast.68, f32[]{:T(128)} %constant.34.clone.1, f32[2048,256]{1,0:T(8,128)} %gather_fusion.4, f32[2048,256]{1,0:T(8,128)S(1)} %gather_fusion.5, f32[256]{0:T(256)S(1)} %copy-done.12, f32[]{:T(128)} %constant.21.clone.1), kind=kCustom, calls=%fused_computation.19 | custom fusion | flops 3670016 | bytes 4458496 | tf_op jit(solution)/shard_map/while/body/eval_jaxpr/scatter-add | solution.py:100
  64.7 2.2 scatter_custom_fusion.1
  66.9 6.0 %all-to-all-start = ((bf16[16,40,256]{2,1,0:T(8,128)(2,1)}), bf16[16,40,256]{2,1,0:T(8,128)(2,1)S(1)}, u32[]{:S(2)}, u32[]{:S(2)}) async-start(bf16[16,40,256]{2,1,0:T(8,128)(2,1)} %bitcast.15), calls=%async_computation | async-start | bytes 655360 | tf_op jit(solution)/shard_map/all_to_all | solution.py:27
  73.0 1.1 fusion.30
  75.1 8.9 %all-to-all-done = bf16[16,40,256]{2,1,0:T(8,128)(2,1)S(1)} async-done(((bf16[16,40,256]{2,1,0:T(8,128)(2,1)}), bf16[16,40,256]{2,1,0:T(8,128)(2,1)S(1)}, u32[]{:S(2)}, u32[]{:S(2)}) %all-to-all-start) | async-done | bytes 327712 | tf_op jit(solution)/shard_map/all_to_all | solution.py:27
  84.3 1.0 fusion.15
  85.3 88.9 %all-reduce.7.cloned.1.call-done = (f32[256,256]{1,0:T(8,128)}, f32[256,256]{1,0:T(8,128)}) async-done(((f32[256,256]{1,0:T(8,128)}, f32[256,256]{1,0:T(8,128)}), (f32[256,256]{1,0:T(8,128)}, f32[256,256]{1,0:T(8,128)})) %all-reduce.7.cloned.1.call-update) | async-done | bytes 524304 | tf_op jit(solution)/shard_map/psum | solution.py:31
  174.3 1.3 fusion.58
  175.9 2.1 fusion.52
  178.0 1.0 convolution_convert_fusion.1
  179.0 5.2 %all-to-all-start.1 = ((bf16[16,40,256]{2,1,0:T(8,128)(2,1)}), bf16[16,40,256]{2,1,0:T(8,128)(2,1)S(1)}, u32[]{:S(2)}, u32[]{:S(2)}) async-start(bf16[16,40,256]{2,1,0:T(8,128)(2,1)} %bitcast.17), calls=%async_computation.1 | async-start | bytes 655360 | tf_op jit(solution)/shard_map/all_to_all | solution.py:27
  184.3 1.2 convolution_add_fusion.2
  185.5 1.2 convolution_convert_fusion
  186.7 2.4 convolution_multiply_fusion
  189.1 6.3 %all-to-all-done.1 = bf16[16,40,256]{2,1,0:T(8,128)(2,1)S(1)} async-done(((bf16[16,40,256]{2,1,0:T(8,128)(2,1)}), bf16[16,40,256]{2,1,0:T(8,128)(2,1)S(1)}, u32[]{:S(2)}, u32[]{:S(2)}) %all-to-all-start.1) | async-done | bytes 327712 | tf_op jit(solution)/shard_map/all_to_all | solution.py:27
  195.4 3.5 all-to-all-start.3
  200.1 1.8 gather_fusion.6
  201.9 1.9 convolution_convert_fusion.3
  203.8 2.0 fusion.29
  205.7 4.3 %all-to-all-done.3 = bf16[16,40,256]{2,1,0:T(8,128)(2,1)S(1)} async-done(((bf16[16,40,256]{2,1,0:T(8,128)(2,1)}), bf16[16,40,256]{2,1,0:T(8,128)(2,1)S(1)}, u32[]{:S(2)}, u32[]{:S(2)}) %all-to-all-start.3) | async-done | bytes 327712 | tf_op jit(solution)/shard_map/all_to_all | solution.py:27
  210.0 1.8 gather_fusion.7
  212.8 8.6 %gather_fusion.8 = f32[2048,256]{1,0:T(8,128)} fusion(f32[256,256]{1,0:T(8,128)S(1)} %fusion.6, s32[2048]{0:T(1024)S(1)} %get-tuple-element.77), kind=kCustom, calls=%fused_computation.8 | custom fusion | bytes 4202496 | tf_op jit(solution)/shard_map/while/body/eval_jaxpr/gather | solution.py:160
  221.3 4.4 %fusion.53 = (f32[256]{0:T(256)S(1)}, f32[2048,256]{1,0:T(8,128)}) fusion(f32[2048,256]{1,0:T(8,128)} %gather_fusion.8, f32[256]{0:T(256)S(1)} %copy-done.12, f32[2048,256]{1,0:T(8,128)} %gather_fusion.4, f32[2048,256]{1,0:T(8,128)S(1)} %gather_fusion.5), kind=kLoop, calls=%fused_computation.120 | loop fusion | flops 5766912 | bytes 8390656 | tf_op jit(solution)/shard_map/while/body/eval_jaxpr/reduce_sum | solution.py:161
  225.7 12.0 %scatter_custom_fusion.4 = f32[256,256]{1,0:T(8,128)S(1)} fusion(s32[2048]{0:T(1024)} %bitcast.69, f32[2048,256]{1,0:T(8,128)} %get-tuple-element.56, f32[]{:T(128)} %constant.21.clone.1), kind=kCustom, calls=%fused_computation.59 | custom fusion | flops 524288 | bytes 262656 | tf_op jit(solution)/shard_map/while/body/eval_jaxpr/scatter-add | solution.py:163
  237.8 12.1 %scatter_custom_fusion.3 = f32[384,256]{1,0:T(8,128)S(1)} fusion(s32[2048]{0:T(1024)} %bitcast.70, f32[2048,256]{1,0:T(8,128)} %get-tuple-element.56, f32[]{:T(128)} %constant.21.clone.1), kind=kCustom, calls=%fused_computation.45 | custom fusion | flops 524288 | bytes 393728 | tf_op jit(solution)/shard_map/while/body/eval_jaxpr/scatter-add | solution.py:162
  252.1 3.3 collective-permute-start.7
  255.4 1.3 collective-permute-start.6
  256.7 1.3 collective-permute-start.5
  258.0 1.3 collective-permute-start.4
  259.3 35.1 %psum.53 = f32[256]{0:T(256)S(1)} all-reduce(f32[256]{0:T(256)S(1)} %get-tuple-element.55), channel_id=1, replica_groups=mesh['groups'=2,'dom'=16] {'dom'}, use_global_device_ids=true, to_apply=%region_14.15 | all-reduce | flops 256 | bytes 2048 | tf_op jit(solution)/shard_map/psum | solution.py:185
  298.9 45.8 %all-reduce.5.cloned.1.call-done = (f32[256,256]{1,0:T(8,128)}, f32[256,256]{1,0:T(8,128)}, f32[256,256]{1,0:T(8,128)}, f32[256,256]{1,0:T(8,128)}) async-done(((f32[256,256]{1,0:T(8,128)}, f32[256,256]{1,0:T(8,128)}, f32[256,256]{1,0:T(8,128)}, f32[256,256]{1,0:T(8,128)}), (f32[256,256]{1,0:T(8,128)}, f32[256,256]{1,0:T(8,128)}, f32[256,256]{1,0:T(8,128)}, ...) | async-done | bytes 1048592 | tf_op jit(solution)/shard_map/psum | solution.py:185
  344.7 1.7 broadcast_multiply_fusion.3
  346.3 1.7 broadcast_multiply_fusion.2
  348.0 1.7 broadcast_multiply_fusion.1
  349.7 1.7 broadcast_multiply_fusion
  (76 shorter events, 13.8 us)
Async XLA Ops:
  7.2 167.1 %copy-start = (f32[256,256]{1,0:T(8,128)S(1)}, f32[256,256]{1,0:T(8,128)}, u32[]{:S(2)}) copy-start(f32[256,256]{1,0:T(8,128)} %param.21) | copy-start | bytes 786436
  7.2 29.0 %copy-start.1 = (bf16[256,256]{1,0:T(8,128)(2,1)S(1)}, bf16[256,256]{1,0:T(8,128)(2,1)}, u32[]{:S(2)}) copy-start(bf16[256,256]{1,0:T(8,128)(2,1)} %param.15) | copy-start | bytes 393220
  7.2 29.0 %copy-start.7 = (bf16[256,256]{1,0:T(8,128)(2,1)S(1)}, bf16[256,256]{1,0:T(8,128)(2,1)}, u32[]{:S(2)}) copy-start(bf16[256,256]{1,0:T(8,128)(2,1)} %param.18) | copy-start | bytes 393220
  9.6 33.6 %collective-permute-start.3 = (bf16[32,256]{1,0:T(8,128)(2,1)S(1)}, bf16[32,256]{1,0:T(8,128)(2,1)S(1)}, u32[]{:S(2)}, u32[]{:S(2)}) collective-permute-start(bf16[32,256]{1,0:T(8,128)(2,1)S(1)} %gather_fusion.3), channel_id=1, source_target_pairs={{8,0},{9,1},{10,2},{11,3},{12,4},{13,5},{14,6},{15,7},{24,16},{25,... | collective-permute-start | bytes 49160 | tf_op jit(solution)/shard_map/ppermute | solution.py:14
  12.4 30.7 %collective-permute-start.1 = (bf16[32,256]{1,0:T(8,128)(2,1)S(1)}, bf16[32,256]{1,0:T(8,128)(2,1)S(1)}, u32[]{:S(2)}, u32[]{:S(2)}) collective-permute-start(bf16[32,256]{1,0:T(8,128)(2,1)S(1)} %gather_fusion.1), channel_id=1, source_target_pairs={{1,0},{2,1},{3,2},{4,3},{5,4},{6,5},{7,6},{8,7},{9,8},{10,9},{11,1... | collective-permute-start | bytes 49160 | tf_op jit(solution)/shard_map/ppermute | solution.py:14
  15.3 27.8 %collective-permute-start = (bf16[32,256]{1,0:T(8,128)(2,1)S(1)}, bf16[32,256]{1,0:T(8,128)(2,1)S(1)}, u32[]{:S(2)}, u32[]{:S(2)}) collective-permute-start(bf16[32,256]{1,0:T(8,128)(2,1)S(1)} %gather_fusion), channel_id=1, source_target_pairs={{0,1},{1,2},{2,3},{3,4},{4,5},{5,6},{6,7},{7,8},{8,9},{9,10},{10,1... | collective-permute-start | bytes 49160 | tf_op jit(solution)/shard_map/ppermute | solution.py:14
  19.8 23.3 %collective-permute-start.2 = (bf16[32,256]{1,0:T(8,128)(2,1)S(1)}, bf16[32,256]{1,0:T(8,128)(2,1)S(1)}, u32[]{:S(2)}, u32[]{:S(2)}) collective-permute-start(bf16[32,256]{1,0:T(8,128)(2,1)S(1)} %gather_fusion.2), channel_id=1, source_target_pairs={{0,8},{1,9},{2,10},{3,11},{4,12},{5,13},{6,14},{7,15},{16,24},{17,... | collective-permute-start | bytes 49160 | tf_op jit(solution)/shard_map/ppermute | solution.py:14
  30.2 36.7 %all-to-all-start.2 = ((bf16[16,40,256]{2,1,0:T(8,128)(2,1)}), bf16[16,40,256]{2,1,0:T(8,128)(2,1)}, u32[]{:S(2)}, u32[]{:S(2)}) async-start(bf16[16,40,256]{2,1,0:T(8,128)(2,1)} %bitcast.19), calls=%async_computation.2 | async-start | bytes 655360 | tf_op jit(solution)/shard_map/all_to_all | solution.py:27
  36.4 6.8 %copy-start.5 = (bf16[256,256]{1,0:T(8,128)(2,1)S(1)}, bf16[256,256]{1,0:T(8,128)(2,1)}, u32[]{:S(2)}) copy-start(bf16[256,256]{1,0:T(8,128)(2,1)} %param.17) | copy-start | bytes 393220
  43.4 8.6 %copy-start.12 = (f32[256]{0:T(256)S(1)}, f32[256]{0:T(256)}, u32[]{:S(2)}) copy-start(f32[256]{0:T(256)} %param.19) | copy-start | bytes 3076
  52.0 21.0 %copy-start.13 = (s32[1,640]{1,0:T(1,128)S(1)}, s32[1,640]{1,0:T(1,128)}, u32[]{:S(2)}) copy-start(s32[1,640]{1,0:T(1,128)} %param.27) | copy-start | bytes 7684
  52.0 22.1 %copy-start.11 = (s32[16]{0:T(128)S(1)}, s32[16]{0:T(128)}, u32[]{:S(2)}) copy-start(s32[16]{0:T(128)} %param.28) | copy-start | bytes 196
  64.6 19.5 %copy-start.4 = (bf16[256,256]{1,0:T(8,128)(2,1)S(1)}, bf16[256,256]{1,0:T(8,128)(2,1)}, u32[]{:S(2)}) copy-start(bf16[256,256]{1,0:T(8,128)(2,1)} %param.20) | copy-start | bytes 393220
  64.7 2.2 copy-start.2
  66.9 17.1 %all-to-all-start = ((bf16[16,40,256]{2,1,0:T(8,128)(2,1)}), bf16[16,40,256]{2,1,0:T(8,128)(2,1)S(1)}, u32[]{:S(2)}, u32[]{:S(2)}) async-start(bf16[16,40,256]{2,1,0:T(8,128)(2,1)} %bitcast.15), calls=%async_computation | async-start | bytes 655360 | tf_op jit(solution)/shard_map/all_to_all | solution.py:27
  72.9 101.4 %all-reduce.7.cloned.1.call-start = ((), (), s32[]{:S(2)}) async-start(), calls=%async_computation.5 | async-start | bytes 1048576 | tf_op jit(solution)/shard_map/psum | solution.py:31
  175.6 3.4 copy-start.9
  179.0 16.3 %all-to-all-start.1 = ((bf16[16,40,256]{2,1,0:T(8,128)(2,1)}), bf16[16,40,256]{2,1,0:T(8,128)(2,1)S(1)}, u32[]{:S(2)}, u32[]{:S(2)}) async-start(bf16[16,40,256]{2,1,0:T(8,128)(2,1)} %bitcast.17), calls=%async_computation.1 | async-start | bytes 655360 | tf_op jit(solution)/shard_map/all_to_all | solution.py:27
  195.4 14.6 %all-to-all-start.3 = ((bf16[16,40,256]{2,1,0:T(8,128)(2,1)}), bf16[16,40,256]{2,1,0:T(8,128)(2,1)S(1)}, u32[]{:S(2)}, u32[]{:S(2)}) async-start(bf16[16,40,256]{2,1,0:T(8,128)(2,1)} %bitcast.64), calls=%async_computation.3 | async-start | bytes 655360 | tf_op jit(solution)/shard_map/all_to_all | solution.py:27
  198.9 145.7 %all-reduce.5.cloned.1.call-start = ((), (), s32[]{:S(2)}) async-start(), calls=%async_computation.4 | async-start | bytes 2097152 | tf_op jit(solution)/shard_map/psum | solution.py:185
  221.3 29.6 %copy-start.6 = (bf16[256,256]{1,0:T(8,128)(2,1)S(1)}, bf16[256,256]{1,0:T(8,128)(2,1)}, u32[]{:S(2)}) copy-start(bf16[256,256]{1,0:T(8,128)(2,1)} %param.17) | copy-start | bytes 393220
  237.8 56.7 %copy-start.3 = (bf16[256,256]{1,0:T(8,128)(2,1)S(1)}, bf16[256,256]{1,0:T(8,128)(2,1)}, u32[]{:S(2)}) copy-start(bf16[256,256]{1,0:T(8,128)(2,1)} %gather_fusion.7) | copy-start | bytes 393220
  237.8 56.7 %copy-start.8 = (bf16[256,256]{1,0:T(8,128)(2,1)S(1)}, bf16[256,256]{1,0:T(8,128)(2,1)}, u32[]{:S(2)}) copy-start(bf16[256,256]{1,0:T(8,128)(2,1)} %param.18) | copy-start | bytes 393220
  252.1 45.9 %collective-permute-start.7 = (bf16[32,256]{1,0:T(8,128)(2,1)S(1)}, bf16[32,256]{1,0:T(8,128)(2,1)S(1)}, u32[]{:S(2)}, u32[]{:S(2)}) collective-permute-start(bf16[32,256]{1,0:T(8,128)(2,1)S(1)} %get-tuple-element.57), channel_id=1, source_target_pairs={{0,8},{1,9},{2,10},{3,11},{4,12},{5,13},{6,14},{7,15},{16,24},{17,... | collective-permute-start | bytes 49160 | tf_op jit(solution)/shard_map/ppermute | solution.py:14
  255.4 41.7 %collective-permute-start.6 = (bf16[32,256]{1,0:T(8,128)(2,1)S(1)}, bf16[32,256]{1,0:T(8,128)(2,1)S(1)}, u32[]{:S(2)}, u32[]{:S(2)}) collective-permute-start(bf16[32,256]{1,0:T(8,128)(2,1)S(1)} %get-tuple-element.68), channel_id=1, source_target_pairs={{8,0},{9,1},{10,2},{11,3},{12,4},{13,5},{14,6},{15,7},{24,16},{25,... | collective-permute-start | bytes 49160 | tf_op jit(solution)/shard_map/ppermute | solution.py:14
  256.7 39.4 %collective-permute-start.5 = (bf16[32,256]{1,0:T(8,128)(2,1)S(1)}, bf16[32,256]{1,0:T(8,128)(2,1)S(1)}, u32[]{:S(2)}, u32[]{:S(2)}) collective-permute-start(bf16[32,256]{1,0:T(8,128)(2,1)S(1)} %get-tuple-element.69), channel_id=1, source_target_pairs={{0,1},{1,2},{2,3},{3,4},{4,5},{5,6},{6,7},{7,8},{8,9},{9,10},{10,1... | collective-permute-start | bytes 49160 | tf_op jit(solution)/shard_map/ppermute | solution.py:14
  258.0 37.2 %collective-permute-start.4 = (bf16[32,256]{1,0:T(8,128)(2,1)S(1)}, bf16[32,256]{1,0:T(8,128)(2,1)S(1)}, u32[]{:S(2)}, u32[]{:S(2)}) collective-permute-start(bf16[32,256]{1,0:T(8,128)(2,1)S(1)} %get-tuple-element.70), channel_id=1, source_target_pairs={{1,0},{2,1},{3,2},{4,3},{5,4},{6,5},{7,6},{8,7},{9,8},{10,9},{11,1... | collective-permute-start | bytes 49160 | tf_op jit(solution)/shard_map/ppermute | solution.py:14
  298.9 52.4 %copy-start.10 = (f32[256,256]{1,0:T(8,128)}, f32[256,256]{1,0:T(8,128)S(1)}, u32[]{:S(2)}) copy-start(f32[256,256]{1,0:T(8,128)S(1)} %scatter_custom_fusion.8) | copy-start | bytes 786436
Sparse Core Ops, SparseCore 0:
  85.4 88.7 all-reduce.6
  252.2 92.3 all-reduce.4
where the time goes:
time: 359 us; the launch traced here: 358 us
  waiting for transfers between devices  154 us (43%)
  other arithmetic  56 us (16%)
  starting transfers between devices  38.6 us (11%)
  local copies, waits for them, and re-layouts  38 us (11%)
  blocking collectives  35.1 us (10%)
  matrix products  21.6 us (6%)
  between operations  14.6 us (4%)
    psum x1, waiting for transfers between devices, top_total(): return lax.psum(partial_value, 'dom')  88.9 us
    psum x1, waiting for transfers between devices, shards(): lax.psum((send_term, recv_term, bias_sum, coarse_term, out_term), 'dom')  45.8 us
    psum x1, blocking collectives, shards(): lax.psum((send_term, recv_term, bias_sum, coarse_term, out_term), 'dom')  35.1 us
    all_to_all x4, waiting for transfers between devices, owner_trade(): lax.all_to_all(buffer, 'dom', split_axis=0, concat_axis=0, tiled=True)  19.5 us
    all_to_all x4, starting transfers between devices, owner_trade(): lax.all_to_all(buffer, 'dom', split_axis=0, concat_axis=0, tiled=True)  19.3 us
    ppermute x8, starting transfers between devices, from_behind(): return lax.ppermute(value, axis, pairs)  19 us
    gather x2, local copies, waits for them, and re-layouts, forward_block(): pre_act = send_proj[block_senders] + recv_proj[block_receivers] + edge_bias  15.2 us
    scatter-add x1, other arithmetic, forward_block(): jax.ops.segment_sum(jax.nn.silu(pre_act), block_receivers, num_segments=l...  12.6 us
  transfers between devices with their start and end apart: 14, of which 5 were waited for; matrix products, arithmetic and copies ran while one was open for 16% of the time, Pallas kernels for 0%

commit v1 on v0

v1 whole, which is shorter than its diff:
```python
import functools

import jax
import jax.numpy as jnp
from jax import lax
from jax.experimental import pallas as pl
from jax.experimental.pallas import tpu as pltpu
from jax.sharding import PartitionSpec as P

DEG = 8
PW = 8
NCC = 256
OFFSETS = (1, -1, PW, -PW)
F32 = jnp.float32
BF16 = jnp.bfloat16


def mm(left, right):
    return lax.dot_general(left, right, (((1,), (0,)), ((), ())), preferred_element_type=F32)


def tn(left, right):
    return lax.dot_general(left, right, (((0,), (0,)), ((), ())), preferred_element_type=F32)


def nt(left, right):
    return lax.dot_general(left, right, (((1,), (1,)), ((), ())), preferred_element_type=F32)


def gate_of(values):
    return 0.5 * jnp.tanh(0.5 * values) + 0.5


def one_hot(ids, count):
    rows = lax.broadcasted_iota(jnp.int32, (count, ids.shape[1]), 0)
    return jnp.where(rows == ids, 1.0, 0.0).astype(BF16)


def kernel(
    domains, cap, block,
    feat, og, sw, rw, bias, cw, tw, ow, es, er, hr, osl, ci, cp,
    updated, fgrad, swg, rwg, bg, cwg, twg, owg,
    hsend, table, hots, sgrad, mt, dj, dpart, dland, dfull, ph, hid, cpart, cland, cfull,
    dhal, hret, wpart, wland, wfull, bmine, bland,
    halo_s, halo_r, ret_s, ret_r, stage_s, stage_r,
):
    me = lax.axis_index("dom")
    n = feat.shape[0]
    slots = hr.shape[2]
    ncd = cp.shape[0]
    nc = ncd * domains
    edges = es.shape[1]
    blocks = edges // block
    wrows = wland.shape[2]
    owners = n // wrows
    gscale = float(n * domains) ** (-0.5)
    top_scale = (NCC / nc) ** 0.5

    def to_peers(action):
        def body(i, carry):
            action(lax.rem(me + i, domains))
            return carry
        lax.fori_loop(1, domains, body, 0)

    def rdma(src, dst, s, r, peer):
        return pltpu.make_async_remote_copy(
            src_ref=src, dst_ref=dst, send_sem=s, recv_sem=r,
            device_id={"dom": peer}, device_id_type=pl.DeviceIdType.MESH,
        )

    def drain(ref, sem):
        pltpu.make_async_copy(ref, ref, sem).wait()

    def rows_of(ref, index, count):
        return ref.at[pl.ds(pl.multiple_of(index * count, count), count)]

    def scatter_start(part, land, k):
        def act(peer):
            rdma(rows_of(part, peer, ncd), land.at[me], stage_s.at[k], stage_r.at[k], peer).start()
        to_peers(act)
        land[me] = part[pl.ds(pl.multiple_of(me * ncd, ncd), ncd), :]

    def gather_start(full, k):
        mine = rows_of(full, me, ncd)

        def act(peer):
            rdma(mine, mine, stage_s.at[k], stage_r.at[k], peer).start()
        to_peers(act)

    def land_wait(land, k):
        drain(land.at[pl.ds(0, domains - 1)], stage_r.at[k])

    def full_wait(full, k):
        drain(full.at[pl.ds(0, (domains - 1) * ncd)], stage_r.at[k])

    def own_rows(full, values):
        full[pl.ds(pl.multiple_of(me * ncd, ncd), ncd), :] = values

    def w_scatter(m, k):
        def body(i, carry):
            peer = lax.rem(me + i, domains)

            @pl.when(peer < owners)
            def _():
                rdma(rows_of(wpart.at[m], peer, wrows), wland.at[m, me],
                     stage_s.at[k], stage_r.at[k], peer).start()
            return carry
        lax.fori_loop(1, domains, body, 0)

        @pl.when(me < owners)
        def _():
            wland[m, me] = wpart[m, pl.ds(pl.multiple_of(me * wrows, wrows), wrows), :]

    def w_gather(m, k, k2):
        @pl.when(me < owners)
        def _():
            drain(wland.at[m, pl.ds(0, domains - 1)], stage_r.at[k])
            total = jnp.sum(wland[m].astype(F32), axis=0)
            wfull[m, pl.ds(pl.multiple_of(me * wrows, wrows), wrows), :] = total.astype(BF16)
            mine = rows_of(wfull.at[m], me, wrows)

            def act(peer):
                rdma(mine, mine, stage_s.at[k2], stage_r.at[k2], peer).start()
            to_peers(act)

    def w_count(m, sem, few):
        if owners == domains:
            drain(wpart.at[m, pl.ds(0, few * wrows)], sem)
        else:
            @pl.when(me < owners)
            def _():
                drain(wpart.at[m, pl.ds(0, (owners - 1) * wrows)], sem)

            @pl.when(me >= owners)
            def _():
                drain(wpart.at[m], sem)

    def w_finish(m, k2, out):
        w_count(m, stage_r.at[k2], owners - 1)
        out[...] = gscale * wfull[m].astype(F32)

    barrier = pltpu.get_barrier_semaphore()
    to_peers(lambda peer: pl.semaphore_signal(
        barrier, inc=1, device_id={"dom": peer}, device_id_type=pl.DeviceIdType.MESH))

    features = feat[...]
    for k in range(4):
        hsend[k] = tn(one_hot(hr[0, k:k + 1, :], n), features).astype(BF16)
    owner = jnp.floor((osl[...].astype(F32) + 0.5) * (1.0 / cap)).astype(jnp.int32)
    mt[...] = one_hot(owner * ncd + ci[...], nc)
    d_joined = nt(og[...], ow[...]).astype(BF16)
    dj[...] = d_joined
    dpart[...] = mm(mt[...], d_joined).astype(BF16)
    tops = lax.broadcasted_iota(jnp.int32, (ncd, NCC), 1)
    own_rows(ph, jnp.where(tops == cp[...], 1.0, 0.0).astype(BF16))
    table[0:n, :] = features

    pl.semaphore_wait(barrier, domains - 1)

    def present(offset):
        other = me + offset
        return jnp.logical_and(other >= 0, other < domains)

    def halo_rows_at(ref, k):
        return ref.at[pl.ds(n + k * slots, slots)]

    for k, offset in enumerate(OFFSETS):
        @pl.when(present(offset))
        def _(k=k, offset=offset):
            rdma(hsend.at[k], halo_rows_at(table, k), halo_s.at[k], halo_r.at[k], me + offset).start()

        @pl.when(jnp.logical_not(present(-offset)))
        def _(k=k):
            table[n + k * slots:n + (k + 1) * slots, :] = jnp.zeros((slots, feat.shape[1]), BF16)
    scatter_start(dpart, dland, 0)
    gather_start(ph, 1)

    own_send = mm(features, sw[...])
    own_recv = mm(features, rw[...]) + bias[...]
    tr = n + 4 * slots
    for b in range(blocks):
        cols = slice(b * block, (b + 1) * block)
        hots[b, 0:tr, :] = one_hot(es[0:1, cols], tr)
        hots[b, tr:tr + n, :] = one_hot(er[0:1, cols], n)

    for k, offset in enumerate(OFFSETS):
        @pl.when(present(-offset))
        def _(k=k):
            drain(halo_rows_at(table, k), halo_r.at[k])
    halo_proj = mm(table[n:tr, :], sw[...])
    proj = jnp.concatenate([own_send, halo_proj, own_recv], axis=0).T.astype(BF16)

    aggregate = jnp.zeros((n, feat.shape[1]), F32)
    for b in range(blocks):
        pre = mm(proj, hots[b])
        gate = gate_of(pre)
        act = pre * gate
        sgrad[b] = (gate + act * (1.0 - gate)).astype(BF16)
        aggregate = aggregate + nt(hots[b, tr:tr + n, :], act.astype(BF16))
    hidden = (features.astype(F32) + aggregate * (1.0 / DEG)).astype(BF16)
    hid[...] = hidden
    cpart[...] = mm(mt[...], hidden).astype(BF16)
    scatter_start(cpart, cland, 2)

    land_wait(dland, 0)
    own_rows(dfull, jnp.sum(dland[...].astype(F32), axis=0).astype(BF16))
    gather_start(dfull, 3)

    land_wait(cland, 2)
    own_rows(cfull, (0.25 * jnp.sum(cland[...].astype(F32), axis=0)).astype(BF16))
    gather_start(cfull, 4)

    full_wait(ph, 1)
    full_wait(dfull, 3)
    parents = ph[...]
    d_out_low = dfull[...]
    d_top_sum = tn(parents, d_out_low)
    full_wait(cfull, 4)

    coarse_low = cfull[...]
    coarse_act = mm(coarse_low, cw[...])
    cgate = gate_of(coarse_act)
    csilu = coarse_act * cgate
    coarse_mid = coarse_low.astype(F32) + csilu
    top_low = (tn(parents, coarse_mid.astype(BF16)) * top_scale).astype(BF16)
    top_w = tw[...].astype(BF16)
    top_act = mm(top_low, top_w)
    tgate = gate_of(top_act)
    tsilu = top_act * tgate
    coarse_out = (coarse_mid + mm(parents, tsilu.astype(BF16))).astype(BF16)
    joined = (hid[...].astype(F32) + tn(mt[...], coarse_out)).astype(BF16)
    wpart[0] = tn(joined, og[...]).astype(BF16)
    w_scatter(0, 5)
    d_top_act = (d_top_sum * (tgate + tsilu * (1.0 - tgate))).astype(BF16)
    d_top = nt(d_top_act, top_w)
    d_mid = d_out_low.astype(F32) + top_scale * mm(parents, d_top.astype(BF16))
    d_act = (d_mid * (cgate + csilu * (1.0 - cgate))).astype(BF16)
    d_coarse = (d_mid + nt(d_act, cw[...])).astype(BF16)
    d_hidden = dj[...].astype(F32) + 0.25 * tn(mt[...], d_coarse)
    fgrad[...] = d_hidden
    d_agg = (d_hidden * (1.0 / DEG)).T.astype(BF16)

    d_proj = jnp.zeros((tr + n, feat.shape[1]), F32)
    for b in range(blocks):
        d_pre = mm(d_agg, hots[b, tr:tr + n, :]) * sgrad[b].astype(F32)
        d_proj = d_proj + nt(hots[b], d_pre.astype(BF16))
    d_send = d_proj[0:tr].astype(BF16)
    d_recv_full = d_proj[tr:tr + n]
    d_recv = d_recv_full.astype(BF16)
    bsum = jnp.sum(d_recv_full, axis=0, keepdims=True)
    bmine[...] = jnp.broadcast_to(bsum, bmine.shape)
    bland[me] = bmine[...]
    to_peers(lambda peer: rdma(bmine, bland.at[me], stage_s.at[7], stage_r.at[7], peer).start())
    wpart[1] = tn(table[...], d_send).astype(BF16)
    w_scatter(1, 8)
    wpart[2] = tn(features, d_recv).astype(BF16)
    w_scatter(2, 10)
    d_table = nt(d_send, sw[...])
    dhal[...] = d_table[n:tr].astype(BF16)
    for k, offset in enumerate(OFFSETS):
        rows = pl.ds(k * slots, slots)

        @pl.when(present(-offset))
        def _(k=k, offset=offset, rows=rows):
            rdma(dhal.at[rows], hret.at[rows], ret_s.at[k], ret_r.at[k], me - offset).start()

        @pl.when(jnp.logical_not(present(offset)))
        def _(k=k):
            hret[k * slots:(k + 1) * slots, :] = jnp.zeros((slots, feat.shape[1]), BF16)

    w_gather(0, 5, 6)
    fgrad[...] += d_table[0:n] + nt(d_recv, rw[...])
    updated[...] = mm(joined, ow[...]).astype(BF16)
    twg[...] = gscale * tn(top_low, d_top_act)
    cwg[...] = gscale * tn(coarse_low, d_act)
    w_gather(1, 8, 9)
    w_gather(2, 10, 11)
    for k, offset in enumerate(OFFSETS):
        @pl.when(present(offset))
        def _(k=k):
            drain(hret.at[pl.ds(k * slots, slots)], ret_r.at[k])
    back = jnp.zeros((n, feat.shape[1]), F32)
    for k in range(4):
        back = back + mm(one_hot(hr[0, k:k + 1, :], n), hret[k * slots:(k + 1) * slots, :])
    fgrad[...] += back
    drain(bland.at[pl.ds(0, domains - 1)], stage_r.at[7])
    bg[...] = gscale * jnp.sum(bland[...], axis=0)[0:1]
    w_finish(0, 6, owg)
    w_finish(1, 9, swg)
    w_finish(2, 11, rwg)

    for k, offset in enumerate(OFFSETS):
        @pl.when(present(offset))
        def _(k=k):
            drain(hsend.at[k], halo_s.at[k])

        @pl.when(present(-offset))
        def _(k=k):
            drain(dhal.at[pl.ds(k * slots, slots)], ret_s.at[k])
    for k in (0, 1, 2, 3, 4):
        full_like = dpart.at[pl.ds(0, (domains - 1) * ncd)]
        drain(full_like, stage_s.at[k])
    drain(bland.at[pl.ds(0, domains - 1)], stage_s.at[7])
    for m, k, k2 in ((0, 5, 6), (1, 8, 9), (2, 10, 11)):
        w_count(m, stage_s.at[k], owners - 1)

        @pl.when(me < owners)
        def _(m=m, k2=k2):
            drain(wland.at[m, pl.ds(0, domains - 1)], stage_s.at[k2])


def shards(
    features, out_grad, send_weight, recv_weight, edge_bias, coarse_weight, top_weight, out_weight,
    edge_sender, edge_receiver, halo_rows, owner_slot, cluster_index, slot_coarse, coarse_parent,
):
    domains = lax.axis_size("dom")
    n, h = features.shape
    ncd = coarse_parent.shape[0]
    nc = ncd * domains
    slots = halo_rows.shape[2]
    tr = n + 4 * slots
    edges = edge_sender.shape[1]
    block = min(edges, 512)
    blocks = edges // block
    cap = slot_coarse.shape[1] // domains
    wrows = max(16, n // domains)
    vmem = pl.BlockSpec(memory_space=pltpu.VMEM)
    dma = pltpu.SemaphoreType.DMA
    scratch = [
        pltpu.VMEM((4, slots, h), BF16),
        pltpu.VMEM((tr, h), BF16),
        pltpu.VMEM((blocks, tr + n, block), BF16),
        pltpu.VMEM((blocks, h, block), BF16),
        pltpu.VMEM((nc, n), BF16),
        pltpu.VMEM((n, h), BF16),
        pltpu.VMEM((nc, h), BF16),
        pltpu.VMEM((domains, ncd, h), BF16),
        pltpu.VMEM((nc, h), BF16),
        pltpu.VMEM((nc, NCC), BF16),
        pltpu.VMEM((n, h), BF16),
        pltpu.VMEM((nc, h), BF16),
        pltpu.VMEM((domains, ncd, h), BF16),
        pltpu.VMEM((nc, h), BF16),
        pltpu.VMEM((4 * slots, h), BF16),
        pltpu.VMEM((4 * slots, h), BF16),
        pltpu.VMEM((3, h, h), BF16),
        pltpu.VMEM((3, domains, wrows, h), BF16),
        pltpu.VMEM((3, h, h), BF16),
        pltpu.VMEM((8, h), F32),
        pltpu.VMEM((domains, 8, h), F32),
        dma((4,)), dma((4,)), dma((4,)), dma((4,)), dma((12,)), dma((12,)),
    ]
    big = jax.ShapeDtypeStruct((h, h), F32)
    outs = pl.pallas_call(
        functools.partial(kernel, domains, cap, block),
        out_shape=(
            jax.ShapeDtypeStruct((n, h), BF16),
            jax.ShapeDtypeStruct((n, h), F32),
            big, big, jax.ShapeDtypeStruct((1, h), F32), big, big, big,
        ),
        in_specs=[vmem] * 14,
        out_specs=[vmem] * 8,
        scratch_shapes=scratch,
        compiler_params=pltpu.CompilerParams(
            collective_id=0, has_side_effects=True, vmem_limit_bytes=56 * 1024 * 1024
        ),
    )(
        features, out_grad, send_weight, recv_weight, edge_bias.reshape(1, h), coarse_weight,
        top_weight, out_weight, edge_sender, edge_receiver, halo_rows, owner_slot, cluster_index,
        coarse_parent.reshape(ncd, 1),
    )
    return outs[:4] + (outs[4].reshape(h),) + outs[5:]


def solution(mesh):
    rows = P(("groups", "dom"), None)
    in_specs = (
        rows, rows, P(), P(), P(), P(), P(), P(), rows, rows,
        P(("groups", "dom"), None, None), rows, rows, rows, P(("groups", "dom")),
    )
    mat = P("groups", None)
    out_specs = (rows, rows, mat, mat, P("groups"), mat, mat, mat)
    return jax.shard_map(shards, mesh=mesh, in_specs=in_specs, out_specs=out_specs, check_vma=False)
```

time: 359 us -> 60 us (0.17)
  waiting for transfers between devices: 154 us -> 0 us
  other arithmetic: 56 us -> 0 us
  Pallas kernels: 0 us -> 50 us
  starting transfers between devices: 38.6 us -> 0 us
  blocking collectives: 35.1 us -> 0 us
  local copies, waits for them, and re-layouts: 38 us -> 9.09 us
  matrix products: 21.6 us -> 0 us
  between operations: 14.6 us -> 0.67 us
    psum x2 -> x0, waiting for transfers between devices: 135 us -> none  [the longest x1 88.9 us: top_total(): return lax.psum(partial_value, 'dom')]
    pallas_call x0 -> x1, Pallas kernels: none -> 50 us  [shards(): pl.pallas_call(functools.partial(kernel, domains, cap, block), out_shape=...]
    scatter-add x7 -> x0, other arithmetic: 40.4 us -> none  [the longest x1 12.6 us: forward_block(): jax.ops.segment_sum(jax.nn.silu(pre_act), block_receivers, num_segments=l...]
    psum x1 -> x0, blocking collectives: 35.1 us -> none  [shards(): lax.psum((send_term, recv_term, bias_sum, coarse_term, out_term), 'dom')]
    gather x9 -> x0, local copies, waits for them, and re-layouts: 33.5 us -> none  [the longest x2 15.2 us: forward_block(): pre_act = send_proj[block_senders] + recv_proj[block_receivers] + edge_bias]
    dot_general x22 -> x0, matrix products: 21.6 us -> none  [the longest x9 10.9 us: contract_first(): lax.dot_general(left, right, (((0,), (0,)), ((), ())), precision=precisio...]
    all_to_all x4 -> x0, waiting for transfers between devices: 19.5 us -> none  [owner_trade(): lax.all_to_all(buffer, 'dom', split_axis=0, concat_axis=0, tiled=True)]
    all_to_all x4 -> x0, starting transfers between devices: 19.3 us -> none  [owner_trade(): lax.all_to_all(buffer, 'dom', split_axis=0, concat_axis=0, tiled=True)]
  transfers between devices with their start and end apart: 14 -> 0, of which waited for: 5 -> 0; matrix products, arithmetic and copies ran while one was open for 16% -> 0% of each run, Pallas kernels for 0% -> 0%
where the time goes in v1:
time: 60 us; the launch traced here: 59.7 us
  Pallas kernels  50 us (83%)
  local copies, waits for them, and re-layouts  9.09 us (15%)
  between operations  0.67 us (1%)
    pallas_call x1, Pallas kernels, shards(): pl.pallas_call(functools.partial(kernel, domains, cap, block), out_shape=...  50 us
    unnamed x24, local copies, waits for them, and re-layouts  8.41 us

profile of v1, /device:TPU:0, one launch (start us, length us, event | category | flops | bytes accessed | tf_op | source)
XLA Modules:
  0.0 59.7 jit_solution(10646319097462805027)
XLA Ops:
  0.6 0.0 copy-start.7
  0.6 0.6 %copy-done.7 = s32[16]{0:T(128)S(1)} copy-done((s32[16]{0:T(128)S(1)}, s32[16]{0:T(128)}, u32[]{:S(2)}) %copy-start.7) | copy-done | bytes 88
  1.3 0.7 %copy.22.cp = s32[16,1]{1,0:T(8,128)} copy(s32[16,1]{0,1:T(1,128)S(1)} %bitcast.5) | data formatting | bytes 128 | tf_op jit(solution)/shard_map/reshape | solution.py:370
  2.0 50.0 %shard_map.197 = (bf16[256,256]{1,0:T(8,128)(2,1)}, f32[256,256]{1,0:T(8,128)}, f32[256,256]{1,0:T(8,128)}, f32[256,256]{1,0:T(8,128)}, f32[1,256]{1,0:T(1,128)}...) custom-call(bf16[256,256]{1,0:T(8,128)(2,1)} %feat.1, bf16[256,256]{1,0:T(8,128)(2,1)} %og.1, ...), custom_call_target="tpu_custom_call" | custom-call | tf_op jit(solution)/shard_map/pallas_call | solution.py:354
  51.9 0.0 copy-start.5
  52.0 1.6 %copy.31 = bf16[256,256]{1,0:T(8,128)(2,1)} copy(bf16[256,256]{1,0:T(8,128)(2,1)} %get-tuple-element.32) | data formatting | bytes 262144
  53.6 0.0 copy-done.5
  53.6 0.0 copy-start.4
  53.6 0.7 %copy.32 = f32[256,256]{1,0:T(8,128)} copy(f32[256,256]{1,0:T(8,128)S(1)} %copy-done.5) | data formatting | bytes 524288
  54.3 0.3 copy-done.4
  54.6 0.0 copy-start.3
  54.6 0.7 %copy.33 = f32[256,256]{1,0:T(8,128)} copy(f32[256,256]{1,0:T(8,128)S(1)} %copy-done.4) | data formatting | bytes 524288
  55.3 0.3 copy-done.3
  55.7 0.0 copy-start.6
  55.7 0.0 copy-start.2
  55.7 0.7 %copy.34 = f32[256,256]{1,0:T(8,128)} copy(f32[256,256]{1,0:T(8,128)S(1)} %copy-done.3) | data formatting | bytes 524288
  56.4 0.0 copy-done.6
  56.4 0.6 copy.35
  56.9 0.0 copy-done.2
  56.9 0.0 copy-start.1
  56.9 0.7 %copy.36 = f32[256,256]{1,0:T(8,128)} copy(f32[256,256]{1,0:T(8,128)S(1)} %copy-done.2) | data formatting | bytes 524288
  57.6 0.3 copy-done.1
  58.0 0.0 copy-start
  58.0 0.7 %copy.37 = f32[256,256]{1,0:T(8,128)} copy(f32[256,256]{1,0:T(8,128)S(1)} %copy-done.1) | data formatting | bytes 524288
  58.7 0.3 copy-done
  59.0 0.7 %copy.38 = f32[256,256]{1,0:T(8,128)} copy(f32[256,256]{1,0:T(8,128)S(1)} %copy-done) | data formatting | bytes 524288
Async XLA Ops:
  0.6 0.7 %copy-start.7 = (s32[16]{0:T(128)S(1)}, s32[16]{0:T(128)}, u32[]{:S(2)}) copy-start(s32[16]{0:T(128)} %param.28) | copy-start | bytes 196
  51.9 1.6 %copy-start.5 = (f32[256,256]{1,0:T(8,128)S(1)}, f32[256,256]{1,0:T(8,128)}, u32[]{:S(2)}) copy-start(f32[256,256]{1,0:T(8,128)} %get-tuple-element.33) | copy-start | bytes 786436
  53.6 1.0 %copy-start.4 = (f32[256,256]{1,0:T(8,128)S(1)}, f32[256,256]{1,0:T(8,128)}, u32[]{:S(2)}) copy-start(f32[256,256]{1,0:T(8,128)} %get-tuple-element.34) | copy-start | bytes 786436
  54.6 1.0 %copy-start.3 = (f32[256,256]{1,0:T(8,128)S(1)}, f32[256,256]{1,0:T(8,128)}, u32[]{:S(2)}) copy-start(f32[256,256]{1,0:T(8,128)} %get-tuple-element.35) | copy-start | bytes 786436
  55.7 0.7 %copy-start.6 = (f32[1,256]{1,0:T(1,128)S(1)}, f32[1,256]{1,0:T(1,128)}, u32[]{:S(2)}) copy-start(f32[1,256]{1,0:T(1,128)} %get-tuple-element.20) | copy-start | bytes 3076
  55.7 1.3 %copy-start.2 = (f32[256,256]{1,0:T(8,128)S(1)}, f32[256,256]{1,0:T(8,128)}, u32[]{:S(2)}) copy-start(f32[256,256]{1,0:T(8,128)} %get-tuple-element.37) | copy-start | bytes 786436
  56.9 1.0 %copy-start.1 = (f32[256,256]{1,0:T(8,128)S(1)}, f32[256,256]{1,0:T(8,128)}, u32[]{:S(2)}) copy-start(f32[256,256]{1,0:T(8,128)} %get-tuple-element.38) | copy-start | bytes 786436
  58.0 1.0 %copy-start = (f32[256,256]{1,0:T(8,128)S(1)}, f32[256,256]{1,0:T(8,128)}, u32[]{:S(2)}) copy-start(f32[256,256]{1,0:T(8,128)} %get-tuple-element.39) | copy-start | bytes 786436

commit v2 on v1

--- a/solution.py
+++ b/solution.py
@@ -27,6 +27,21 @@
     return lax.dot_general(left, right, (((1,), (1,)), ((), ())), preferred_element_type=F32)
 
 
+def halves(values):
+    high = values.astype(BF16)
+    return high, (values - high.astype(F32)).astype(BF16)
+
+
+def mm_exact(hot, values):
+    high, low = halves(values)
+    return mm(hot, high) + mm(hot, low)
+
+
+def tn_exact(hot, values):
+    high, low = halves(values)
+    return tn(hot, high) + tn(hot, low)
+
+
 def gate_of(values):
     return 0.5 * jnp.tanh(0.5 * values) + 0.5
 
@@ -39,15 +54,15 @@
 def kernel(
     domains, cap, block,
     feat, og, sw, rw, bias, cw, tw, ow, es, er, hr, osl, ci, cp,
-    updated, fgrad, swg, rwg, bg, cwg, twg, owg,
+    updated, fgrad, wfull, bg, cwg, twg,
     hsend, table, hots, sgrad, mt, dj, dpart, dland, dfull, ph, hid, cpart, cland, cfull,
-    dhal, hret, wpart, wland, wfull, bmine, bland,
+    dhal, hret, wpart, wland, bmine, bland,
     halo_s, halo_r, ret_s, ret_r, stage_s, stage_r,
 ):
     me = lax.axis_index("dom")
     n = feat.shape[0]
     slots = hr.shape[2]
-    ncd = cp.shape[0]
+    ncd = cp.shape[1]
     nc = ncd * domains
     edges = es.shape[1]
     blocks = edges // block
@@ -135,9 +150,8 @@
             def _():
                 drain(wpart.at[m], sem)
 
-    def w_finish(m, k2, out):
+    def w_finish(m, k2):
         w_count(m, stage_r.at[k2], owners - 1)
-        out[...] = gscale * wfull[m].astype(F32)
 
     barrier = pltpu.get_barrier_semaphore()
     to_peers(lambda peer: pl.semaphore_signal(
@@ -151,8 +165,8 @@
     d_joined = nt(og[...], ow[...]).astype(BF16)
     dj[...] = d_joined
     dpart[...] = mm(mt[...], d_joined).astype(BF16)
-    tops = lax.broadcasted_iota(jnp.int32, (ncd, NCC), 1)
-    own_rows(ph, jnp.where(tops == cp[...], 1.0, 0.0).astype(BF16))
+    values = lax.broadcasted_iota(jnp.int32, (NCC, 128), 0).astype(F32).astype(BF16)
+    own_rows(ph, tn(one_hot(cp[...], NCC), values).astype(BF16))
     table[0:n, :] = features
 
     pl.semaphore_wait(barrier, domains - 1)
@@ -207,33 +221,39 @@
     gather_start(dfull, 3)
 
     land_wait(cland, 2)
-    own_rows(cfull, (0.25 * jnp.sum(cland[...].astype(F32), axis=0)).astype(BF16))
+    own_rows(cfull, 0.25 * jnp.sum(cland[...].astype(F32), axis=0))
     gather_start(cfull, 4)
 
     full_wait(ph, 1)
     full_wait(dfull, 3)
-    parents = ph[...]
-    d_out_low = dfull[...]
-    d_top_sum = tn(parents, d_out_low)
+    lanes = lax.broadcasted_iota(jnp.int32, (nc, NCC), 1).astype(F32)
+    ids = ph[...].astype(F32)
+    ids = jnp.concatenate([ids] * (NCC // 128), axis=1)
+    parents = jnp.where(lanes == ids, 1.0, 0.0).astype(BF16)
+    d_out = dfull[...].astype(F32)
+    d_top_sum = tn(parents, dfull[...])
     full_wait(cfull, 4)
 
-    coarse_low = cfull[...]
+    coarse = cfull[...]
+    coarse_low = coarse.astype(BF16)
     coarse_act = mm(coarse_low, cw[...])
     cgate = gate_of(coarse_act)
     csilu = coarse_act * cgate
-    coarse_mid = coarse_low.astype(F32) + csilu
-    top_low = (tn(parents, coarse_mid.astype(BF16)) * top_scale).astype(BF16)
-    top_w = tw[...].astype(BF16)
-    top_act = mm(top_low, top_w)
+    coarse_mid = coarse + csilu
+    top_level = tn_exact(parents, coarse_mid) * top_scale
+    top_hi, top_lo = halves(top_level)
+    w_hi, w_lo = halves(tw[...])
+    top_act = mm(top_hi, w_hi) + (mm(top_hi, w_lo) + mm(top_lo, w_hi))
     tgate = gate_of(top_act)
     tsilu = top_act * tgate
-    coarse_out = (coarse_mid + mm(parents, tsilu.astype(BF16))).astype(BF16)
+    coarse_out = (coarse_mid + mm_exact(parents, tsilu)).astype(BF16)
     joined = (hid[...].astype(F32) + tn(mt[...], coarse_out)).astype(BF16)
     wpart[0] = tn(joined, og[...]).astype(BF16)
     w_scatter(0, 5)
-    d_top_act = (d_top_sum * (tgate + tsilu * (1.0 - tgate))).astype(BF16)
-    d_top = nt(d_top_act, top_w)
-    d_mid = d_out_low.astype(F32) + top_scale * mm(parents, d_top.astype(BF16))
+    d_top_act = d_top_sum * (tgate + tsilu * (1.0 - tgate))
+    dt_hi, dt_lo = halves(d_top_act)
+    d_top = nt(dt_hi, w_hi) + (nt(dt_hi, w_lo) + nt(dt_lo, w_hi))
+    d_mid = d_out + top_scale * mm_exact(parents, d_top)
     d_act = (d_mid * (cgate + csilu * (1.0 - cgate))).astype(BF16)
     d_coarse = (d_mid + nt(d_act, cw[...])).astype(BF16)
     d_hidden = dj[...].astype(F32) + 0.25 * tn(mt[...], d_coarse)
@@ -248,7 +268,7 @@
     d_recv_full = d_proj[tr:tr + n]
     d_recv = d_recv_full.astype(BF16)
     bsum = jnp.sum(d_recv_full, axis=0, keepdims=True)
-    bmine[...] = jnp.broadcast_to(bsum, bmine.shape)
+    bmine[...] = bsum
     bland[me] = bmine[...]
     to_peers(lambda peer: rdma(bmine, bland.at[me], stage_s.at[7], stage_r.at[7], peer).start())
     wpart[1] = tn(table[...], d_send).astype(BF16)
@@ -271,7 +291,7 @@
     w_gather(0, 5, 6)
     fgrad[...] += d_table[0:n] + nt(d_recv, rw[...])
     updated[...] = mm(joined, ow[...]).astype(BF16)
-    twg[...] = gscale * tn(top_low, d_top_act)
+    twg[...] = gscale * (tn(top_hi, dt_hi) + (tn(top_hi, dt_lo) + tn(top_lo, dt_hi)))
     cwg[...] = gscale * tn(coarse_low, d_act)
     w_gather(1, 8, 9)
     w_gather(2, 10, 11)
@@ -284,10 +304,10 @@
         back = back + mm(one_hot(hr[0, k:k + 1, :], n), hret[k * slots:(k + 1) * slots, :])
     fgrad[...] += back
     drain(bland.at[pl.ds(0, domains - 1)], stage_r.at[7])
-    bg[...] = gscale * jnp.sum(bland[...], axis=0)[0:1]
-    w_finish(0, 6, owg)
-    w_finish(1, 9, swg)
-    w_finish(2, 11, rwg)
+    bg[...] = gscale * jnp.sum(bland[...], axis=0)
+    w_finish(0, 6)
+    w_finish(1, 9)
+    w_finish(2, 11)
 
     for k, offset in enumerate(OFFSETS):
         @pl.when(present(offset))
@@ -297,9 +317,8 @@
         @pl.when(present(-offset))
         def _(k=k):
             drain(dhal.at[pl.ds(k * slots, slots)], ret_s.at[k])
-    for k in (0, 1, 2, 3, 4):
-        full_like = dpart.at[pl.ds(0, (domains - 1) * ncd)]
-        drain(full_like, stage_s.at[k])
+    for ref, k in ((dpart, 0), (ph, 1), (cpart, 2), (dfull, 3), (cfull, 4)):
+        drain(ref.at[pl.ds(0, (domains - 1) * ncd)], stage_s.at[k])
     drain(bland.at[pl.ds(0, domains - 1)], stage_s.at[7])
     for m, k, k2 in ((0, 5, 6), (1, 8, 9), (2, 10, 11)):
         w_count(m, stage_s.at[k], owners - 1)
@@ -307,6 +326,20 @@
         @pl.when(me < owners)
         def _(m=m, k2=k2):
             drain(wland.at[m, pl.ds(0, domains - 1)], stage_s.at[k2])
+
+
+def finish(
+    gscale, updated_in, fgrad_in, wfull, bias_in, coarse_in, top_in,
+    updated, fgrad, swg, rwg, bg, cwg, twg, owg,
+):
+    updated[...] = updated_in[...]
+    fgrad[...] = fgrad_in[...]
+    owg[...] = gscale * wfull[0].astype(F32)
+    swg[...] = gscale * wfull[1].astype(F32)
+    rwg[...] = gscale * wfull[2].astype(F32)
+    bg[...] = bias_in[...]
+    cwg[...] = coarse_in[...]
+    twg[...] = top_in[...]
 
 
 def shards(
@@ -336,18 +369,17 @@
         pltpu.VMEM((nc, h), BF16),
         pltpu.VMEM((domains, ncd, h), BF16),
         pltpu.VMEM((nc, h), BF16),
-        pltpu.VMEM((nc, NCC), BF16),
+        pltpu.VMEM((nc, 128), BF16),
         pltpu.VMEM((n, h), BF16),
         pltpu.VMEM((nc, h), BF16),
         pltpu.VMEM((domains, ncd, h), BF16),
-        pltpu.VMEM((nc, h), BF16),
+        pltpu.VMEM((nc, h), F32),
         pltpu.VMEM((4 * slots, h), BF16),
         pltpu.VMEM((4 * slots, h), BF16),
         pltpu.VMEM((3, h, h), BF16),
         pltpu.VMEM((3, domains, wrows, h), BF16),
-        pltpu.VMEM((3, h, h), BF16),
-        pltpu.VMEM((8, h), F32),
-        pltpu.VMEM((domains, 8, h), F32),
+        pltpu.VMEM((1, h), F32),
+        pltpu.VMEM((domains, 1, h), F32),
         dma((4,)), dma((4,)), dma((4,)), dma((4,)), dma((12,)), dma((12,)),
     ]
     big = jax.ShapeDtypeStruct((h, h), F32)
@@ -356,10 +388,10 @@
         out_shape=(
             jax.ShapeDtypeStruct((n, h), BF16),
             jax.ShapeDtypeStruct((n, h), F32),
-            big, big, jax.ShapeDtypeStruct((1, h), F32), big, big, big,
+            jax.ShapeDtypeStruct((3, h, h), BF16), jax.ShapeDtypeStruct((1, h), F32), big, big,
         ),
         in_specs=[vmem] * 14,
-        out_specs=[vmem] * 8,
+        out_specs=[vmem] * 6,
         scratch_shapes=scratch,
         compiler_params=pltpu.CompilerParams(
             collective_id=0, has_side_effects=True, vmem_limit_bytes=56 * 1024 * 1024
@@ -367,8 +399,19 @@
     )(
         features, out_grad, send_weight, recv_weight, edge_bias.reshape(1, h), coarse_weight,
         top_weight, out_weight, edge_sender, edge_receiver, halo_rows, owner_slot, cluster_index,
-        coarse_parent.reshape(ncd, 1),
+        coarse_parent.reshape(1, ncd),
     )
+    outs = pl.pallas_call(
+        functools.partial(finish, float(n * domains) ** (-0.5)),
+        out_shape=(
+            jax.ShapeDtypeStruct((n, h), BF16),
+            jax.ShapeDtypeStruct((n, h), F32),
+            big, big, jax.ShapeDtypeStruct((1, h), F32), big, big, big,
+        ),
+        in_specs=[vmem] * 6,
+        out_specs=[vmem] * 8,
+        compiler_params=pltpu.CompilerParams(vmem_limit_bytes=60 * 1024 * 1024),
+    )(*outs)
     return outs[:4] + (outs[4].reshape(h),) + outs[5:]
 
 

time: 60 us -> 52 us (0.87)
  local copies, waits for them, and re-layouts: 9.09 us -> 0 us
  Pallas kernels: 50 us -> 51.2 us
    unnamed x24 -> x0, local copies, waits for them, and re-layouts: 8.41 us -> none
    pallas_call x0 -> x1, Pallas kernels: none -> 2.5 us  [shards(): pl.pallas_call(functools.partial(finish, float(n * domains) ** (-0.5)), o...]
    pallas_call x1, Pallas kernels: 50 us -> 48.7 us  [shards(): pl.pallas_call(functools.partial(kernel, domains, cap, block), out_shape=...]
    reshape x1 -> x0, local copies, waits for them, and re-layouts: 0.68 us -> none  [shards(): coarse_parent.reshape(ncd, 1)]
where the time goes in v2:
time: 52 us; the launch traced here: 51.9 us
  Pallas kernels  51.2 us (98%)
  between operations  0.65 us (1%)
    pallas_call x1, Pallas kernels, shards(): pl.pallas_call(functools.partial(kernel, domains, cap, block), out_shape=...  48.7 us
    pallas_call x1, Pallas kernels, shards(): pl.pallas_call(functools.partial(finish, float(n * domains) ** (-0.5)), o...  2.5 us

profile of v2, /device:TPU:0, one launch (start us, length us, event | category | flops | bytes accessed | tf_op | source)
XLA Modules:
  0.0 51.9 jit_solution(9367908304591047301)
XLA Ops:
  0.6 48.7 %shard_map.197 = (bf16[256,256]{1,0:T(8,128)(2,1)}, f32[256,256]{1,0:T(8,128)}, bf16[3,256,256]{2,1,0:T(8,128)(2,1)}, f32[1,256]{1,0:T(1,128)}, f32[256,256]{1,0:T(8,128)}, /*index=5*/f32[256,256]{1,0:T(8,128)}) custom-call(bf16[256,256]{1,0:T(8,128)(2,1)} %feat.1, bf16[256,256]{1,0:T(8,128)(2,1)} %og.1, bf16[256,256]{1,0:T(8,128)(2,1)} %sw.1, ...), custom_call_target="tpu_custom_call" | custom-call | tf_op jit(solution)/shard_map/pallas_call | solution.py:386
  49.4 2.5 %shard_map.198 = (bf16[256,256]{1,0:T(8,128)(2,1)}, f32[256,256]{1,0:T(8,128)}, f32[256,256]{1,0:T(8,128)}, f32[256,256]{1,0:T(8,128)}, f32[1,256]{1,0:T(1,128)}...) custom-call(bf16[256,256]{1,0:T(8,128)(2,1)} %get-tuple-element.22.updated_in, ...), custom_call_target="tpu_custom_call" | custom-call | tf_op jit(solution)/shard_map/pallas_call | solution.py:404

commit v3 on v2

v3 whole, which is shorter than its diff:
```python
import functools

import jax
import jax.numpy as jnp
from jax import lax
from jax.experimental import pallas as pl
from jax.experimental.pallas import tpu as pltpu
from jax.sharding import PartitionSpec as P

DEG = 8
PW = 8
NCC = 256
OFFSETS = (1, -1, PW, -PW)
F32 = jnp.float32
BF16 = jnp.bfloat16


def mm(left, right):
    return lax.dot_general(left, right, (((1,), (0,)), ((), ())), preferred_element_type=F32)


def tn(left, right):
    return lax.dot_general(left, right, (((0,), (0,)), ((), ())), preferred_element_type=F32)


def nt(left, right):
    return lax.dot_general(left, right, (((1,), (1,)), ((), ())), preferred_element_type=F32)


def halves(values):
    high = values.astype(BF16)
    return high, (values - high.astype(F32)).astype(BF16)


def mm_exact(hot, values):
    high, low = halves(values)
    return mm(hot, high) + mm(hot, low)


def tn_exact(hot, values):
    high, low = halves(values)
    return tn(hot, high) + tn(hot, low)


def gate_of(values):
    return 0.5 * jnp.tanh(0.5 * values) + 0.5


def one_hot(ids, count):
    rows = lax.broadcasted_iota(jnp.int32, (count, ids.shape[1]), 0)
    return jnp.where(rows == ids, 1.0, 0.0).astype(BF16)


def kernel(
    domains, cap, block,
    feat, og, sw, rw, bias, cw, tw, ow, es, er, hr, osl, ci, cp,
    updated, fgrad, wf0, wf1, wf2, bg, cwg, twg,
    hsend, table, hots, sgrad, mt, dj, dpart, dpl, dps, dland, dfull, ph, hid, cpart, cpl, cps, cland, cfull,
    dhal, hret, wp0, wp1, wp2, wq0, wq1, wq2, ws0, ws1, ws2, wl0, wl1, wl2, bmine, bland,
    halo_s, halo_r, ret_s, ret_r, stage_s, stage_r,
):
    me = lax.axis_index("dom")
    n = feat.shape[0]
    slots = hr.shape[2]
    ncd = cp.shape[1]
    h = feat.shape[1]
    wrows = wl0.shape[1]
    wparts, wplands, wpsums = (wp0, wp1, wp2), (wq0, wq1, wq2), (ws0, ws1, ws2)
    wlands, wfulls = (wl0, wl1, wl2), (wf0, wf1, wf2)
    nc = ncd * domains
    edges = es.shape[1]
    blocks = edges // block
    gscale = float(n * domains) ** (-0.5)
    top_scale = (NCC / nc) ** 0.5

    def to_peers(action):
        def body(i, carry):
            action(lax.rem(me + i, domains))
            return carry
        lax.fori_loop(1, domains, body, 0)

    def rdma(src, dst, s, r, peer):
        return pltpu.make_async_remote_copy(
            src_ref=src, dst_ref=dst, send_sem=s, recv_sem=r,
            device_id={"dom": peer}, device_id_type=pl.DeviceIdType.MESH,
        )

    def drain(ref, sem):
        pltpu.make_async_copy(ref, ref, sem).wait()

    half = domains // 2
    slot = lax.div(me, 2)
    par = lax.rem(me, 2)
    partner = me + 1 - 2 * par
    wown = h // wrows // 2

    def piece(start, count):
        return pl.ds(pl.multiple_of(start * count, count), count)

    def if_owner(oh, action):
        if oh == half:
            action()
        else:
            pl.when(slot < oh)(action)

    def same_parity(action):
        def body(i, carry):
            other = lax.rem(slot + i, half)
            action(other, 2 * other + par)
            return carry
        lax.fori_loop(1, half, body, 0)

    def pair_start(part, pland, k):
        rows = pland.shape[0]
        rdma(part.at[piece(1 - par, rows)], pland, stage_s.at[4 * k], stage_r.at[4 * k], partner).start()

    def scatter_start(part, pland, psum, land, k, oh):
        rows, count = pland.shape[0], land.shape[1]
        drain(pland, stage_r.at[4 * k])
        psum[...] = (part[piece(par, rows), :] + pland[...]).astype(BF16)

        def act(other, peer):
            def go():
                rdma(psum.at[piece(other, count)], land.at[slot],
                     stage_s.at[4 * k + 1], stage_r.at[4 * k + 1], peer).start()
            if oh == half:
                go()
            else:
                pl.when(other < oh)(go)
        same_parity(act)

        def own():
            land[slot] = psum[piece(slot, count), :]
        if_owner(oh, own)

    def land_sum(land, k):
        drain(land.at[pl.ds(0, half - 1)], stage_r.at[4 * k + 1])
        return jnp.sum(land[...].astype(F32), axis=0)

    def gather_start(full, values, k, oh):
        count = values.shape[0]
        index = par * oh + slot
        full[piece(index, count), :] = values
        mine = full.at[piece(index, count)]
        same_parity(lambda other, peer: rdma(
            mine, mine, stage_s.at[4 * k + 2], stage_r.at[4 * k + 2], peer).start())

    def block_drain(ref, sem, oh, count):
        if oh == half:
            drain(ref.at[pl.ds(0, (oh - 1) * count)], sem)
        else:
            @pl.when(slot < oh)
            def _():
                drain(ref.at[pl.ds(0, (oh - 1) * count)], sem)

            @pl.when(slot >= oh)
            def _():
                drain(ref.at[pl.ds(0, oh * count)], sem)

    def forward(full, k, oh, count):
        rows = oh * count
        block_drain(full, stage_r.at[4 * k + 2], oh, count)
        mine = full.at[piece(par, rows)]
        rdma(mine, mine, stage_s.at[4 * k + 3], stage_r.at[4 * k + 3], partner).start()

    def full_wait(full, k, oh, count):
        drain(full.at[pl.ds(0, oh * count)], stage_r.at[4 * k + 3])

    def w_gather(m):
        def act():
            gather_start(wfulls[m], land_sum(wlands[m], 2 + m).astype(BF16), 2 + m, wown)
        if_owner(wown, act)

    barrier = pltpu.get_barrier_semaphore()
    to_peers(lambda peer: pl.semaphore_signal(
        barrier, inc=1, device_id={"dom": peer}, device_id_type=pl.DeviceIdType.MESH))

    features = feat[...]
    for k in range(4):
        hsend[k] = tn(one_hot(hr[0, k:k + 1, :], n), features).astype(BF16)
    owner = jnp.floor((osl[...].astype(F32) + 0.5) * (1.0 / cap))
    chip = jnp.floor(owner * 0.5)
    place = (owner - 2.0 * chip) * half + chip
    mt[...] = one_hot(place.astype(jnp.int32) * ncd + ci[...], nc)
    d_joined = nt(og[...], ow[...]).astype(BF16)
    dj[...] = d_joined
    dpart[...] = mm(mt[...], d_joined)
    values = lax.broadcasted_iota(jnp.int32, (NCC, 128), 0).astype(F32).astype(BF16)
    my_parents = tn(one_hot(cp[...], NCC), values).astype(BF16)
    table[0:n, :] = features

    pl.semaphore_wait(barrier, domains - 1)

    def present(offset):
        other = me + offset
        return jnp.logical_and(other >= 0, other < domains)

    def halo_rows_at(ref, k):
        return ref.at[pl.ds(n + k * slots, slots)]

    for k, offset in enumerate(OFFSETS):
        @pl.when(present(offset))
        def _(k=k, offset=offset):
            rdma(hsend.at[k], halo_rows_at(table, k), halo_s.at[k], halo_r.at[k], me + offset).start()

        @pl.when(jnp.logical_not(present(-offset)))
        def _(k=k):
            table[n + k * slots:n + (k + 1) * slots, :] = jnp.zeros((slots, feat.shape[1]), BF16)
    pair_start(dpart, dpl, 0)
    gather_start(ph, my_parents, 5, half)

    own_send = mm(features, sw[...])
    own_recv = mm(features, rw[...]) + bias[...]
    tr = n + 4 * slots
    for b in range(blocks):
        cols = slice(b * block, (b + 1) * block)
        hots[b, 0:tr, :] = one_hot(es[0:1, cols], tr)
        hots[b, tr:tr + n, :] = one_hot(er[0:1, cols], n)

    scatter_start(dpart, dpl, dps, dland, 0, half)
    for k, offset in enumerate(OFFSETS):
        @pl.when(present(-offset))
        def _(k=k):
            drain(halo_rows_at(table, k), halo_r.at[k])
    halo_proj = mm(table[n:tr, :], sw[...])
    proj = jnp.concatenate([own_send, halo_proj, own_recv], axis=0).T.astype(BF16)

    aggregate = jnp.zeros((n, feat.shape[1]), F32)
    for b in range(blocks):
        pre = mm(proj, hots[b])
        gate = gate_of(pre)
        act = pre * gate
        sgrad[b] = (gate + act * (1.0 - gate)).astype(BF16)
        aggregate = aggregate + nt(hots[b, tr:tr + n, :], act.astype(BF16))
    hidden = (features.astype(F32) + aggregate * (1.0 / DEG)).astype(BF16)
    hid[...] = hidden
    cpart[...] = mm(mt[...], hidden)
    pair_start(cpart, cpl, 1)
    forward(ph, 5, half, ncd)
    d_own = land_sum(dland, 0).astype(BF16)
    scatter_start(cpart, cpl, cps, cland, 1, half)
    gather_start(dfull, d_own, 0, half)
    gather_start(cfull, 0.25 * land_sum(cland, 1), 1, half)
    forward(dfull, 0, half, ncd)
    full_wait(ph, 5, half, ncd)
    lanes = lax.broadcasted_iota(jnp.int32, (nc, NCC), 1).astype(F32)
    ids = ph[...].astype(F32)
    ids = jnp.concatenate([ids] * (NCC // 128), axis=1)
    parents = jnp.where(lanes == ids, 1.0, 0.0).astype(BF16)
    full_wait(dfull, 0, half, ncd)
    forward(cfull, 1, half, ncd)
    d_out = dfull[...].astype(F32)
    d_top_sum = tn(parents, dfull[...])
    full_wait(cfull, 1, half, ncd)

    coarse = cfull[...]
    coarse_low = coarse.astype(BF16)
    coarse_act = mm(coarse_low, cw[...])
    cgate = gate_of(coarse_act)
    csilu = coarse_act * cgate
    coarse_mid = coarse + csilu
    top_level = tn_exact(parents, coarse_mid) * top_scale
    top_hi, top_lo = halves(top_level)
    w_hi, w_lo = halves(tw[...])
    top_act = mm(top_hi, w_hi) + (mm(top_hi, w_lo) + mm(top_lo, w_hi))
    tgate = gate_of(top_act)
    tsilu = top_act * tgate
    coarse_out = (coarse_mid + mm_exact(parents, tsilu)).astype(BF16)
    joined = (hid[...].astype(F32) + tn(mt[...], coarse_out)).astype(BF16)
    wp0[...] = tn(joined, og[...])
    pair_start(wp0, wq0, 2)
    d_top_act = d_top_sum * (tgate + tsilu * (1.0 - tgate))
    dt_hi, dt_lo = halves(d_top_act)
    d_top = nt(dt_hi, w_hi) + (nt(dt_hi, w_lo) + nt(dt_lo, w_hi))
    d_mid = d_out + top_scale * mm_exact(parents, d_top)
    d_act = (d_mid * (cgate + csilu * (1.0 - cgate))).astype(BF16)
    d_coarse = (d_mid + nt(d_act, cw[...])).astype(BF16)
    scatter_start(wparts[0], wplands[0], wpsums[0], wlands[0], 2 + 0, wown)
    d_hidden = dj[...].astype(F32) + 0.25 * tn(mt[...], d_coarse)
    fgrad[...] = d_hidden
    d_agg = (d_hidden * (1.0 / DEG)).T.astype(BF16)

    d_proj = jnp.zeros((tr + n, feat.shape[1]), F32)
    for b in range(blocks):
        d_pre = mm(d_agg, hots[b, tr:tr + n, :]) * sgrad[b].astype(F32)
        d_proj = d_proj + nt(hots[b], d_pre.astype(BF16))
    d_send = d_proj[0:tr].astype(BF16)
    d_recv_full = d_proj[tr:tr + n]
    d_recv = d_recv_full.astype(BF16)
    bsum = jnp.sum(d_recv_full, axis=0, keepdims=True)
    bmine[...] = bsum
    bland[me] = bmine[...]
    to_peers(lambda peer: rdma(bmine, bland.at[me], stage_s.at[24], stage_r.at[24], peer).start())
    wp1[...] = tn(table[...], d_send)
    pair_start(wp1, wq1, 3)
    wp2[...] = tn(features, d_recv)
    pair_start(wp2, wq2, 4)
    d_table = nt(d_send, sw[...])
    dhal[...] = d_table[n:tr].astype(BF16)
    for k, offset in enumerate(OFFSETS):
        rows = pl.ds(k * slots, slots)

        @pl.when(present(-offset))
        def _(k=k, offset=offset, rows=rows):
            rdma(dhal.at[rows], hret.at[rows], ret_s.at[k], ret_r.at[k], me - offset).start()

        @pl.when(jnp.logical_not(present(offset)))
        def _(k=k):
            hret[k * slots:(k + 1) * slots, :] = jnp.zeros((slots, feat.shape[1]), BF16)

    scatter_start(wparts[1], wplands[1], wpsums[1], wlands[1], 2 + 1, wown)
    scatter_start(wparts[2], wplands[2], wpsums[2], wlands[2], 2 + 2, wown)
    w_gather(0)
    fgrad[...] += d_table[0:n] + nt(d_recv, rw[...])
    updated[...] = mm(joined, ow[...]).astype(BF16)
    twg[...] = gscale * (tn(top_hi, dt_hi) + (tn(top_hi, dt_lo) + tn(top_lo, dt_hi)))
    cwg[...] = gscale * tn(coarse_low, d_act)
    w_gather(1)
    w_gather(2)
    forward(wf0, 2, wown, wrows)
    for k, offset in enumerate(OFFSETS):
        @pl.when(present(offset))
        def _(k=k):
            drain(hret.at[pl.ds(k * slots, slots)], ret_r.at[k])
    back = jnp.zeros((n, feat.shape[1]), F32)
    for k in range(4):
        back = back + mm(one_hot(hr[0, k:k + 1, :], n), hret[k * slots:(k + 1) * slots, :])
    fgrad[...] += back
    drain(bland.at[pl.ds(0, domains - 1)], stage_r.at[24])
    bg[...] = gscale * jnp.sum(bland[...], axis=0)
    forward(wf1, 3, wown, wrows)
    forward(wf2, 4, wown, wrows)
    for m in range(3):
        full_wait(wfulls[m], 2 + m, wown, wrows)

    for k, offset in enumerate(OFFSETS):
        @pl.when(present(offset))
        def _(k=k):
            drain(hsend.at[k], halo_s.at[k])

        @pl.when(present(-offset))
        def _(k=k):
            drain(dhal.at[pl.ds(k * slots, slots)], ret_s.at[k])
    stages = [(dpl, dps, dland, dfull, half, ncd, 0), (cpl, cps, cland, cfull, half, ncd, 1)]
    for m in range(3):
        stages.append((wplands[m], wpsums[m], wlands[m], wfulls[m], wown, wrows, 2 + m))
    for pland, psum, land, full, oh, count, k in stages:
        drain(pland, stage_s.at[4 * k])
        block_drain(psum, stage_s.at[4 * k + 1], oh, count)
    stages.append((None, None, None, ph, half, ncd, 5))
    for pland, psum, land, full, oh, count, k in stages:
        def sent(full=full, land=land, oh=oh, count=count, k=k):
            if oh == half:
                drain(full.at[pl.ds(0, (half - 1) * count)], stage_s.at[4 * k + 2])
            else:
                drain(land.at[pl.ds(0, half - 1)], stage_s.at[4 * k + 2])
        if_owner(oh, sent)
        drain(full.at[pl.ds(0, oh * count)], stage_s.at[4 * k + 3])
    drain(bland.at[pl.ds(0, domains - 1)], stage_s.at[24])


def finish(
    gscale, updated_in, fgrad_in, w0, w1, w2, bias_in, coarse_in, top_in,
    updated, fgrad, swg, rwg, bg, cwg, twg, owg,
):
    updated[...] = updated_in[...]
    fgrad[...] = fgrad_in[...]
    owg[...] = gscale * w0[...].astype(F32)
    swg[...] = gscale * w1[...].astype(F32)
    rwg[...] = gscale * w2[...].astype(F32)
    bg[...] = bias_in[...]
    cwg[...] = coarse_in[...]
    twg[...] = top_in[...]


def shards(
    features, out_grad, send_weight, recv_weight, edge_bias, coarse_weight, top_weight, out_weight,
    edge_sender, edge_receiver, halo_rows, owner_slot, cluster_index, slot_coarse, coarse_parent,
):
    domains = lax.axis_size("dom")
    n, h = features.shape
    ncd = coarse_parent.shape[0]
    nc = ncd * domains
    slots = halo_rows.shape[2]
    tr = n + 4 * slots
    edges = edge_sender.shape[1]
    block = min(edges, 512)
    blocks = edges // block
    cap = slot_coarse.shape[1] // domains
    wrows = max(16, h // domains)
    vmem = pl.BlockSpec(memory_space=pltpu.VMEM)
    dma = pltpu.SemaphoreType.DMA
    scratch = [
        pltpu.VMEM((4, slots, h), BF16),
        pltpu.VMEM((tr, h), BF16),
        pltpu.VMEM((blocks, tr + n, block), BF16),
        pltpu.VMEM((blocks, h, block), BF16),
        pltpu.VMEM((nc, n), BF16),
        pltpu.VMEM((n, h), BF16),
        pltpu.VMEM((nc, h), F32),
        pltpu.VMEM((nc // 2, h), F32),
        pltpu.VMEM((nc // 2, h), BF16),
        pltpu.VMEM((domains // 2, ncd, h), BF16),
        pltpu.VMEM((nc, h), BF16),
        pltpu.VMEM((nc, 128), BF16),
        pltpu.VMEM((n, h), BF16),
        pltpu.VMEM((nc, h), F32),
        pltpu.VMEM((nc // 2, h), F32),
        pltpu.VMEM((nc // 2, h), BF16),
        pltpu.VMEM((domains // 2, ncd, h), BF16),
        pltpu.VMEM((nc, h), F32),
        pltpu.VMEM((4 * slots, h), BF16),
        pltpu.VMEM((4 * slots, h), BF16),
        *[pltpu.VMEM((h, h), F32)] * 3,
        *[pltpu.VMEM((h // 2, h), F32)] * 3,
        *[pltpu.VMEM((h // 2, h), BF16)] * 3,
        *[pltpu.VMEM((domains // 2, wrows, h), BF16)] * 3,
        pltpu.VMEM((1, h), F32),
        pltpu.VMEM((domains, 1, h), F32),
        dma((4,)), dma((4,)), dma((4,)), dma((4,)), dma((25,)), dma((25,)),
    ]
    big = jax.ShapeDtypeStruct((h, h), F32)
    outs = pl.pallas_call(
        functools.partial(kernel, domains, cap, block),
        out_shape=(
            jax.ShapeDtypeStruct((n, h), BF16),
            jax.ShapeDtypeStruct((n, h), F32),
            *[jax.ShapeDtypeStruct((h, h), BF16)] * 3, jax.ShapeDtypeStruct((1, h), F32), big, big,
        ),
        in_specs=[vmem] * 14,
        out_specs=[vmem] * 8,
        scratch_shapes=scratch,
        compiler_params=pltpu.CompilerParams(
            collective_id=0, has_side_effects=True, vmem_limit_bytes=56 * 1024 * 1024
        ),
    )(
        features, out_grad, send_weight, recv_weight, edge_bias.reshape(1, h), coarse_weight,
        top_weight, out_weight, edge_sender, edge_receiver, halo_rows, owner_slot, cluster_index,
        coarse_parent.reshape(1, ncd),
    )
    outs = pl.pallas_call(
        functools.partial(finish, float(n * domains) ** (-0.5)),
        out_shape=(
            jax.ShapeDtypeStruct((n, h), BF16),
            jax.ShapeDtypeStruct((n, h), F32),
            big, big, jax.ShapeDtypeStruct((1, h), F32), big, big, big,
        ),
        in_specs=[vmem] * 8,
        out_specs=[vmem] * 8,
        compiler_params=pltpu.CompilerParams(vmem_limit_bytes=60 * 1024 * 1024),
    )(*outs)
    return outs[:4] + (outs[4].reshape(h),) + outs[5:]


def solution(mesh):
    rows = P(("groups", "dom"), None)
    in_specs = (
        rows, rows, P(), P(), P(), P(), P(), P(), rows, rows,
        P(("groups", "dom"), None, None), rows, rows, rows, P(("groups", "dom")),
    )
    mat = P("groups", None)
    out_specs = (rows, rows, mat, mat, P("groups"), mat, mat, mat)
    return jax.shard_map(shards, mesh=mesh, in_specs=in_specs, out_specs=out_specs, check_vma=False)
```

time: 52 us -> 46.3 us (0.89)
  Pallas kernels: 51.2 us -> 45.5 us
    pallas_call x1, Pallas kernels: 48.7 us -> 42.9 us  [shards(): pl.pallas_call(functools.partial(kernel, domains, cap, block), out_shape=...]
where the time goes in v3:
time: 46.3 us; the launch traced here: 46.1 us
  Pallas kernels  45.5 us (98%)
  between operations  0.65 us (1%)
    pallas_call x1, Pallas kernels, shards(): pl.pallas_call(functools.partial(kernel, domains, cap, block), out_shape=...  42.9 us
    pallas_call x1, Pallas kernels, shards(): pl.pallas_call(functools.partial(finish, float(n * domains) ** (-0.5)), o...  2.53 us

profile of v3, /device:TPU:0, one launch (start us, length us, event | category | flops | bytes accessed | tf_op | source)
XLA Modules:
  0.0 46.1 jit_solution(2828367074969651226)
XLA Ops:
  0.6 42.9 %shard_map.197 = (bf16[256,256]{1,0:T(8,128)(2,1)}, f32[256,256]{1,0:T(8,128)}, bf16[256,256]{1,0:T(8,128)(2,1)}, bf16[256,256]{1,0:T(8,128)(2,1)}, bf16[256,256...) custom-call(bf16[256,256]{1,0:T(8,128)(2,1)} %feat.1, bf16[256,256]{1,0:T(8,128)(2,1)} %og.1, ...), custom_call_target="tpu_custom_call" | custom-call | tf_op jit(solution)/shard_map/pallas_call | solution.py:423
  43.6 2.5 %shard_map.198 = (bf16[256,256]{1,0:T(8,128)(2,1)}, f32[256,256]{1,0:T(8,128)}, f32[256,256]{1,0:T(8,128)}, f32[256,256]{1,0:T(8,128)}, f32[1,256]{1,0:T(1,128)}...) custom-call(bf16[256,256]{1,0:T(8,128)(2,1)} %get-tuple-element.24.updated_in, ...), custom_call_target="tpu_custom_call" | custom-call | tf_op jit(solution)/shard_map/pallas_call | solution.py:441

commit v4 on v3

--- a/solution.py
+++ b/solution.py
@@ -225,6 +225,7 @@
     halo_proj = mm(table[n:tr, :], sw[...])
     proj = jnp.concatenate([own_send, halo_proj, own_recv], axis=0).T.astype(BF16)
 
+    gather_start(dfull, land_sum(dland, 0).astype(BF16), 0, half)
     aggregate = jnp.zeros((n, feat.shape[1]), F32)
     for b in range(blocks):
         pre = mm(proj, hots[b])
@@ -237,11 +238,9 @@
     cpart[...] = mm(mt[...], hidden)
     pair_start(cpart, cpl, 1)
     forward(ph, 5, half, ncd)
-    d_own = land_sum(dland, 0).astype(BF16)
+    forward(dfull, 0, half, ncd)
     scatter_start(cpart, cpl, cps, cland, 1, half)
-    gather_start(dfull, d_own, 0, half)
     gather_start(cfull, 0.25 * land_sum(cland, 1), 1, half)
-    forward(dfull, 0, half, ncd)
     full_wait(ph, 5, half, ncd)
     lanes = lax.broadcasted_iota(jnp.int32, (nc, NCC), 1).astype(F32)
     ids = ph[...].astype(F32)

time: 46.3 us -> 48.6 us (1.050)
  Pallas kernels: 45.5 us -> 47.8 us
    pallas_call x1, Pallas kernels: 42.9 us -> 45.3 us  [shards(): pl.pallas_call(functools.partial(kernel, domains, cap, block), out_shape=...]
where the time goes in v4:
time: 48.6 us; the launch traced here: 48.5 us
  Pallas kernels  47.8 us (98%)
  between operations  0.65 us (1%)
    pallas_call x1, Pallas kernels, shards(): pl.pallas_call(functools.partial(kernel, domains, cap, block), out_shape=...  45.3 us
    pallas_call x1, Pallas kernels, shards(): pl.pallas_call(functools.partial(finish, float(n * domains) ** (-0.5)), o...  2.53 us

profile of v4, /device:TPU:0, one launch (start us, length us, event | category | flops | bytes accessed | tf_op | source)
XLA Modules:
  0.0 48.5 jit_solution(15889756017566341614)
XLA Ops:
  0.6 45.3 %shard_map.197 = (bf16[256,256]{1,0:T(8,128)(2,1)}, f32[256,256]{1,0:T(8,128)}, bf16[256,256]{1,0:T(8,128)(2,1)}, bf16[256,256]{1,0:T(8,128)(2,1)}, bf16[256,256...) custom-call(bf16[256,256]{1,0:T(8,128)(2,1)} %feat.1, bf16[256,256]{1,0:T(8,128)(2,1)} %og.1, ...), custom_call_target="tpu_custom_call" | custom-call | tf_op jit(solution)/shard_map/pallas_call | solution.py:422
  45.9 2.5 %shard_map.198 = (bf16[256,256]{1,0:T(8,128)(2,1)}, f32[256,256]{1,0:T(8,128)}, f32[256,256]{1,0:T(8,128)}, f32[256,256]{1,0:T(8,128)}, f32[1,256]{1,0:T(1,128)}...) custom-call(bf16[256,256]{1,0:T(8,128)(2,1)} %get-tuple-element.24.updated_in, ...), custom_call_target="tpu_custom_call" | custom-call | tf_op jit(solution)/shard_map/pallas_call | solution.py:440
